TPU v7x, 32 devices: a whole 2x2x4 slice. The times are simulated.
32 devices in a mesh: rep: 8 (over z, x), fsdp: 4 (over y, core).
Axes of the slice: x: 2, y: 2, z: 4, core: 2. Of those that a mesh axis runs over, the one named last changes fastest.
Arguments:
- tokens: bfloat16 [8, 2048, 1024], P('rep', 'fsdp'), may hold values from -6 to 6
- segments: int32 [8, 2048], P('rep'), may hold values from 0 to 5, never falling along the last dimension, each value on 1 to 512 neighbouring positions
- cotangent: bfloat16 [8, 2048, 1024], P('rep', 'fsdp'), may hold values from -6 to 6
- attn_gain: bfloat16 [1024], P('fsdp'), may hold values from 0.5 to 1.5
- query_weight: bfloat16 [1024, 2048], P('fsdp'), may hold values from -0.1875 to 0.1875
- key_weight: bfloat16 [1024, 1024], P('fsdp'), may hold values from -0.1875 to 0.1875
- value_weight: bfloat16 [1024, 1024], P('fsdp'), may hold values from -0.1875 to 0.1875
- query_gain: bfloat16 [128], P('fsdp'), may hold values from 0.5 to 1.5
- key_gain: bfloat16 [128], P('fsdp'), may hold values from 0.5 to 1.5
- out_weight: bfloat16 [2048, 1024], P('fsdp'), may hold values from -0.75 to 0.75
- mlp_gain: bfloat16 [1024], P('fsdp'), may hold values from 0.5 to 1.5
- gate_weight: bfloat16 [1024, 3072], P('fsdp'), may hold values from -0.1875 to 0.1875
- up_weight: bfloat16 [1024, 3072], P('fsdp'), may hold values from -0.1875 to 0.1875
- down_weight: bfloat16 [3072, 1024], P('fsdp'), may hold values from -0.109375 to 0.109375
Outputs:
- output: bfloat16 [8, 2048, 1024], P('rep', 'fsdp')
- tokens_grad: float32 [8, 2048, 1024], P('rep', 'fsdp')
- attn_gain_grad: float32 [1024], P('fsdp')
- query_weight_grad: float32 [1024, 2048], P('fsdp')
- key_weight_grad: float32 [1024, 1024], P('fsdp')
- value_weight_grad: float32 [1024, 1024], P('fsdp')
- query_gain_grad: float32 [128], P('fsdp')
- key_gain_grad: float32 [128], P('fsdp')
- out_weight_grad: float32 [2048, 1024], P('fsdp')
- mlp_gain_grad: float32 [1024], P('fsdp')
- gate_weight_grad: float32 [1024, 3072], P('fsdp')
- up_weight_grad: float32 [1024, 3072], P('fsdp')
- down_weight_grad: float32 [3072, 1024], P('fsdp')
Inputs may be any that keep to these rules, and one draw needn't show every extreme that they name: `segments`: segment numbers never fall along a sequence; each of the 6 documents of a sequence has 1 to 512 tokens, and one has exactly 512.
All inputs are finite; a program needn't handle non-finite values.
Results may differ from a plain program's by a relative error of at most 0.02.
Values may be sent and summed in bfloat16 or wider, within the bound.
A program may use at most 192 MiB of HBM per device.

v0:
```python
import jax
import jax.numpy as jnp
from jax import lax
from jax.sharding import PartitionSpec as P

EPSILON = 1e-06
ROPE_BASE = 1000000.0
MASKED = -1e30


def passed_along(value, axis, steps):
    count = lax.axis_size(axis)
    first, last = (max(0, -steps), min(count, count - steps))
    return lax.ppermute(value, axis, [(source, source + steps) for source in range(first, last)])


def shortened(shard):
    return jax.tree.map(lambda a: a.astype(jnp.bfloat16) if a.dtype == jnp.float32 else a, shard)


def rms_scale(field, scaling):
    return field * lax.rsqrt(jnp.mean(field * field, axis=-1, keepdims=True) + EPSILON) * scaling


def rotate(field, cosine, sine):
    half_width = field.shape[-1] // 2
    first = field[..., :half_width]
    second = field[..., half_width:]
    return jnp.concatenate(
        [first * cosine - second * sine, second * cosine + first * sine], axis=-1
    )


def rope_tables(positions, head_width):
    freqs = ROPE_BASE ** (-(jnp.arange(head_width // 2, dtype=jnp.float32) * 2.0 / head_width))
    angle_table = positions[:, None] * freqs[None, :]
    return (jnp.cos(angle_table)[:, None, :], jnp.sin(angle_table)[:, None, :])


def gating(gate, upper):
    return jax.nn.silu(gate) * upper


def body(
    tokens,
    segments,
    cotangent,
    attn_gain,
    query_weight,
    key_weight,
    value_weight,
    query_gain,
    key_gain,
    out_weight,
    mlp_gain,
    gate_weight,
    up_weight,
    down_weight,
):
    gathered = (
        lax.all_gather(attn_gain, "fsdp", axis=0, tiled=True),
        lax.all_gather(query_weight, "fsdp", axis=0, tiled=True),
        lax.all_gather(key_weight, "fsdp", axis=0, tiled=True),
        lax.all_gather(value_weight, "fsdp", axis=0, tiled=True),
        lax.all_gather(query_gain, "fsdp", axis=0, tiled=True),
        lax.all_gather(key_gain, "fsdp", axis=0, tiled=True),
        lax.all_gather(out_weight, "fsdp", axis=0, tiled=True),
        lax.all_gather(mlp_gain, "fsdp", axis=0, tiled=True),
        lax.all_gather(gate_weight, "fsdp", axis=0, tiled=True),
        lax.all_gather(up_weight, "fsdp", axis=0, tiled=True),
        lax.all_gather(down_weight, "fsdp", axis=0, tiled=True),
    )
    (
        attn_full,
        wquery,
        wkey,
        wvalue,
        qgain_full,
        kgain_full,
        wout,
        mlp_full,
        wgate,
        wupper,
        wdown,
    ) = gathered
    tok_rows = tokens.shape[1]
    head_dim = qgain_full.shape[0]
    heads = wquery.shape[1] // head_dim
    kv_heads = wkey.shape[1] // head_dim
    group = heads // kv_heads
    span = min(tok_rows, 512)
    scale = head_dim ** (-0.5)
    place = lax.axis_index("fsdp")
    inputs = tokens[0].astype(jnp.float32)
    positions = (place * tok_rows + jnp.arange(tok_rows, dtype=jnp.int32)).astype(jnp.float32)
    cosine, sine = rope_tables(positions, head_dim)
    padded_seg = jnp.concatenate([jnp.full((span,), -1, jnp.int32), segments[0]])
    window_seg = lax.dynamic_slice_in_dim(padded_seg, place * tok_rows, span + tok_rows)
    query_seg = window_seg[span:]
    key_offsets = jnp.arange(2 * span, dtype=jnp.int32)
    query_offsets = jnp.arange(span, dtype=jnp.int32)
    causal = key_offsets[None, :] - span <= query_offsets[:, None]
    masks = [(window_seg[None, 0 : 2 * span] == query_seg[0:span, None]) & causal]
    normed, pull_attn = jax.vjp(rms_scale, inputs, attn_full.astype(jnp.float32))
    act = normed.astype(jnp.bfloat16)
    query_raw = jnp.dot(act, wquery, preferred_element_type=jnp.float32).reshape(
        tok_rows, heads, head_dim
    )
    key_raw = jnp.dot(act, wkey, preferred_element_type=jnp.float32).reshape(
        tok_rows, kv_heads, head_dim
    )
    value = jnp.dot(act, wvalue, preferred_element_type=jnp.float32).astype(jnp.bfloat16)

    def prepare(raw, scaling):
        return rotate(rms_scale(raw, scaling), cosine, sine)

    query_turned, pull_query = jax.vjp(prepare, query_raw, qgain_full.astype(jnp.float32))
    key_turned, pull_key = jax.vjp(prepare, key_raw, kgain_full.astype(jnp.float32))
    query = query_turned.astype(jnp.bfloat16).reshape(tok_rows, heads * head_dim)
    key = key_turned.astype(jnp.bfloat16).reshape(tok_rows, kv_heads * head_dim)
    key_tail, value_tail = passed_along((key, value), "fsdp", 1)
    key_window = jnp.concatenate([key_tail, key], axis=0)
    value_window = jnp.concatenate([value_tail, value], axis=0)
    query_heads = query.reshape(tok_rows, kv_heads, group, head_dim).transpose(1, 2, 0, 3)
    key_heads = key_window.reshape(span + tok_rows, kv_heads, head_dim).transpose(1, 0, 2)
    value_heads = value_window.reshape(span + tok_rows, kv_heads, head_dim).transpose(1, 0, 2)

    def forward_head(operands):
        query_part, key_part, value_part = operands
        scores = (
            jnp.einsum("gqd,kd->gqk", query_part, key_part, preferred_element_type=jnp.float32)
            * scale
        )
        scores = jnp.where(masks[0], scores, MASKED)
        highest = jnp.max(scores, axis=-1, keepdims=True)
        expd = jnp.exp(scores - highest)
        total = jnp.sum(expd, axis=-1, keepdims=True)
        probs = (expd / total).astype(jnp.bfloat16)
        results = [jnp.einsum("gqk,kd->gqd", probs, value_part, preferred_element_type=jnp.float32)]
        totals = [highest[..., 0] + jnp.log(total[..., 0])]
        return (jnp.concatenate(results, axis=1), jnp.concatenate(totals, axis=1))

    attended, log_totals = lax.map(forward_head, (query_heads, key_heads, value_heads))
    mixed = attended.transpose(2, 0, 1, 3).reshape(tok_rows, heads * head_dim).astype(jnp.bfloat16)
    hidden = inputs + jnp.dot(mixed, wout, preferred_element_type=jnp.float32)
    normed2, pull_mlp = jax.vjp(rms_scale, hidden, mlp_full.astype(jnp.float32))
    act2 = normed2.astype(jnp.bfloat16)
    gate = jnp.dot(act2, wgate, preferred_element_type=jnp.float32)
    upper = jnp.dot(act2, wupper, preferred_element_type=jnp.float32)
    inner_f, pull_gate = jax.vjp(gating, gate, upper)
    inner = inner_f.astype(jnp.bfloat16)
    final = (hidden + jnp.dot(inner, wdown, preferred_element_type=jnp.float32)).astype(
        jnp.bfloat16
    )
    wquery, wkey, wvalue, wout, wgate, wupper, wdown = (
        lax.all_gather(query_weight, "fsdp", axis=0, tiled=True),
        lax.all_gather(key_weight, "fsdp", axis=0, tiled=True),
        lax.all_gather(value_weight, "fsdp", axis=0, tiled=True),
        lax.all_gather(out_weight, "fsdp", axis=0, tiled=True),
        lax.all_gather(gate_weight, "fsdp", axis=0, tiled=True),
        lax.all_gather(up_weight, "fsdp", axis=0, tiled=True),
        lax.all_gather(down_weight, "fsdp", axis=0, tiled=True),
    )
    grad_out = cotangent[0]
    down_grad = jnp.einsum("tf,td->fd", inner, grad_out, preferred_element_type=jnp.float32)
    inner_grad = jnp.einsum("td,fd->tf", grad_out, wdown, preferred_element_type=jnp.float32)
    gate_back, upper_back = pull_gate(inner_grad)
    gate_back = gate_back.astype(jnp.bfloat16)
    upper_back = upper_back.astype(jnp.bfloat16)
    gate_grad = jnp.einsum("td,tf->df", act2, gate_back, preferred_element_type=jnp.float32)
    upper_grad = jnp.einsum("td,tf->df", act2, upper_back, preferred_element_type=jnp.float32)
    act2_grad = jnp.einsum(
        "tf,df->td", gate_back, wgate, preferred_element_type=jnp.float32
    ) + jnp.einsum("tf,df->td", upper_back, wupper, preferred_element_type=jnp.float32)
    hidden_norm_grad, mlp_gain_part = pull_mlp(act2_grad)
    hidden_grad = grad_out.astype(jnp.float32) + hidden_norm_grad
    branch_grad = hidden_grad.astype(jnp.bfloat16)
    out_grad = jnp.einsum("te,td->ed", mixed, branch_grad, preferred_element_type=jnp.float32)
    mixed_grad = jnp.einsum(
        "td,ed->te", branch_grad, wout, preferred_element_type=jnp.float32
    ).astype(jnp.bfloat16)
    mixed_heads = mixed_grad.reshape(tok_rows, kv_heads, group, head_dim).transpose(1, 2, 0, 3)

    def backward_head(operands):
        query_part, key_part, value_part, grad_part, total_part = operands
        key_accum = jnp.zeros((key_part.shape[0], head_dim), jnp.float32)
        value_accum = jnp.zeros((key_part.shape[0], head_dim), jnp.float32)
        total_block = total_part[:, 0:span]
        scores = (
            jnp.einsum("gqd,kd->gqk", query_part, key_part, preferred_element_type=jnp.float32)
            * scale
        )
        scores = jnp.where(masks[0], scores, MASKED)
        probs = jnp.exp(scores - total_block[..., None])
        probs_grad = jnp.einsum(
            "gqd,kd->gqk", grad_part, value_part, preferred_element_type=jnp.float32
        )
        centre = jnp.sum(probs_grad * probs, axis=-1, keepdims=True)
        scores_grad = (probs * (probs_grad - centre)).astype(jnp.bfloat16)
        query_grads = [
            jnp.einsum("gqk,kd->gqd", scores_grad, key_part, preferred_element_type=jnp.float32)
            * scale
        ]
        key_accum = key_accum.at[0 : 2 * span].add(
            jnp.einsum("gqk,gqd->kd", scores_grad, query_part, preferred_element_type=jnp.float32)
            * scale
        )
        value_accum = value_accum.at[0 : 2 * span].add(
            jnp.einsum(
                "gqk,gqd->kd",
                probs.astype(jnp.bfloat16),
                grad_part,
                preferred_element_type=jnp.float32,
            )
        )
        return (jnp.concatenate(query_grads, axis=1), key_accum, value_accum)

    query_heads_grad, key_heads_grad, value_heads_grad = lax.map(
        backward_head, (query_heads, key_heads, value_heads, mixed_heads, log_totals)
    )
    query_grad = query_heads_grad.transpose(2, 0, 1, 3).reshape(tok_rows, heads, head_dim)
    key_window_grad = key_heads_grad.transpose(1, 0, 2).reshape(
        span + tok_rows, kv_heads * head_dim
    )
    value_window_grad = value_heads_grad.transpose(1, 0, 2).reshape(
        span + tok_rows, kv_heads * head_dim
    )
    key_return, value_return = (
        passed_along(key_window_grad[:span].astype(jnp.bfloat16), "fsdp", -1).astype(jnp.float32),
        passed_along(value_window_grad[:span].astype(jnp.bfloat16), "fsdp", -1).astype(jnp.float32),
    )
    key_own = key_window_grad[span:].at[tok_rows - span :].add(key_return)
    value_own = value_window_grad[span:].at[tok_rows - span :].add(value_return)
    query_raw_grad, query_gain_part = pull_query(query_grad)
    key_raw_grad, key_gain_part = pull_key(key_own.reshape(tok_rows, kv_heads, head_dim))
    query_back = query_raw_grad.reshape(tok_rows, heads * head_dim).astype(jnp.bfloat16)
    key_back = key_raw_grad.reshape(tok_rows, kv_heads * head_dim).astype(jnp.bfloat16)
    value_back = value_own.astype(jnp.bfloat16)
    wquery_grad = jnp.einsum("td,te->de", act, query_back, preferred_element_type=jnp.float32)
    wkey_grad = jnp.einsum("td,te->de", act, key_back, preferred_element_type=jnp.float32)
    wvalue_grad = jnp.einsum("td,te->de", act, value_back, preferred_element_type=jnp.float32)
    act_grad = jnp.einsum("te,de->td", query_back, wquery, preferred_element_type=jnp.float32)
    act_grad = act_grad + jnp.einsum(
        "te,de->td", key_back, wkey, preferred_element_type=jnp.float32
    )
    act_grad = act_grad + jnp.einsum(
        "te,de->td", value_back, wvalue, preferred_element_type=jnp.float32
    )
    input_norm_grad, attn_gain_part = pull_attn(act_grad)
    inputs_grad = hidden_grad + input_norm_grad
    owned = (
        lax.psum_scatter(
            attn_gain_part.astype(jnp.bfloat16), "fsdp", scatter_dimension=0, tiled=True
        ).astype(jnp.float32),
        lax.psum_scatter(
            wquery_grad.astype(jnp.bfloat16), "fsdp", scatter_dimension=0, tiled=True
        ).astype(jnp.float32),
        lax.psum_scatter(
            wkey_grad.astype(jnp.bfloat16), "fsdp", scatter_dimension=0, tiled=True
        ).astype(jnp.float32),
        lax.psum_scatter(
            wvalue_grad.astype(jnp.bfloat16), "fsdp", scatter_dimension=0, tiled=True
        ).astype(jnp.float32),
        lax.psum_scatter(
            query_gain_part.astype(jnp.bfloat16), "fsdp", scatter_dimension=0, tiled=True
        ).astype(jnp.float32),
        lax.psum_scatter(
            key_gain_part.astype(jnp.bfloat16), "fsdp", scatter_dimension=0, tiled=True
        ).astype(jnp.float32),
        lax.psum_scatter(
            out_grad.astype(jnp.bfloat16), "fsdp", scatter_dimension=0, tiled=True
        ).astype(jnp.float32),
        lax.psum_scatter(
            mlp_gain_part.astype(jnp.bfloat16), "fsdp", scatter_dimension=0, tiled=True
        ).astype(jnp.float32),
        lax.psum_scatter(
            gate_grad.astype(jnp.bfloat16), "fsdp", scatter_dimension=0, tiled=True
        ).astype(jnp.float32),
        lax.psum_scatter(
            upper_grad.astype(jnp.bfloat16), "fsdp", scatter_dimension=0, tiled=True
        ).astype(jnp.float32),
        lax.psum_scatter(
            down_grad.astype(jnp.bfloat16), "fsdp", scatter_dimension=0, tiled=True
        ).astype(jnp.float32),
    )
    summed = tuple(
        jax.tree.map(
            lambda part: part.astype(jnp.float32), lax.psum(shortened(tuple(owned)), "rep")
        )
    )
    return (final[None], inputs_grad[None]) + summed


def solution(mesh):
    in_specs = (
        P("rep", "fsdp", None),
        P("rep", None),
        P("rep", "fsdp", None),
        P("fsdp"),
        P("fsdp", None),
        P("fsdp", None),
        P("fsdp", None),
        P("fsdp"),
        P("fsdp"),
        P("fsdp", None),
        P("fsdp"),
        P("fsdp", None),
        P("fsdp", None),
        P("fsdp", None),
    )
    out_specs = (
        P("rep", "fsdp", None),
        P("rep", "fsdp", None),
        P("fsdp"),
        P("fsdp", None),
        P("fsdp", None),
        P("fsdp", None),
        P("fsdp"),
        P("fsdp"),
        P("fsdp", None),
        P("fsdp"),
        P("fsdp", None),
        P("fsdp", None),
        P("fsdp", None),
    )
    return jax.shard_map(body, mesh=mesh, in_specs=in_specs, out_specs=out_specs, check_vma=False)
```

profile of v0, /device:TPU:0, one launch (start us, length us, event | category | flops | bytes accessed | tf_op | source)
XLA Modules:
  0.0 1123.7 jit_solution(1451560726943321244)
XLA Ops:
  11.3 6.0 all-gather
  19.1 8.1 all-reduce.14
  28.1 7.0 all-gather.12.cloned.1.call-done
  35.0 3.9 copy.58
  46.2 14.0 %all-gather.14.cloned.1.call-done = bf16[1024,1024]{1,0:T(8,128)(2,1)} async-done(((bf16[256,1024]{1,0:T(8,128)(2,1)}), bf16[1024,1024]{1,0:T(8,128)(2,1)}) %all-gather.14.cloned.1.call-update) | async-done | bytes 2097168 | tf_op jit(solution)/shard_map/all_gather | solution.py:64
  60.2 3.9 convolution_convert_fusion.8
  67.2 6.8 all-gather.1
  79.4 3.3 bitcast_bitcast_fusion
  82.6 21.8 %all-gather.10.cloned.1.call-done = bf16[1024,2048]{1,0:T(8,128)(2,1)} async-done(((bf16[256,2048]{1,0:T(8,128)(2,1)}), bf16[1024,2048]{1,0:T(8,128)(2,1)}) %all-gather.10.cloned.1.call-update) | async-done | bytes 4194320 | tf_op jit(solution)/shard_map/all_gather | solution.py:62
  104.4 6.4 copy.55
  110.8 4.7 multiply_reduce_fusion.3
  124.3 4.1 maximum_bitcast_fusion
  128.4 56.2 %while.39 = (s32[]{:T(128)}, bf16[8,2,512,128]{2,3,1,0:T(8,128)(2,1)}, f32[8,2,512]{2,1,0:T(2,128)S(1)}, bf16[8,2,512,128]{3,2,1,0:T(8,128)(2,1)}, bf16[8,1024,1...) while((s32[]{:T(128)}, ...), condition=%wide.region_6.7_spmd.clone, body=%wide.region_3.6_spmd.clone.sunk | while | flops 551025664 | bytes 16035945 | solution.py:143
  132.2 3.2 fusion.169
  139.2 3.2 fusion.169
  146.3 3.2 fusion.169
  153.3 3.3 fusion.169
  160.3 3.2 fusion.169
  167.3 3.2 fusion.169
  174.3 3.2 fusion.169
  181.4 3.2 fusion.169
  184.6 5.3 multiply_reduce_fusion.8
  191.9 8.3 fusion.108
  200.2 39.5 %all-gather.20.cloned.1.call-done = bf16[1024,3072]{1,0:T(8,128)(2,1)} async-done(((bf16[256,3072]{1,0:T(8,128)(2,1)}), bf16[1024,3072]{1,0:T(8,128)(2,1)}) %all-gather.20.cloned.1.call-update) | async-done | bytes 6291472 | tf_op jit(solution)/shard_map/all_gather | solution.py:70
  239.7 8.0 fusion.109
  247.8 39.9 %all-gather.22.cloned.1.call-done = bf16[3072,1024]{1,0:T(8,128)(2,1)} async-done(((bf16[768,1024]{1,0:T(8,128)(2,1)}), bf16[3072,1024]{1,0:T(8,128)(2,1)}) %all-gather.22.cloned.1.call-update) | async-done | bytes 6291472 | tf_op jit(solution)/shard_map/all_gather | solution.py:71
  287.7 11.8 %multiply_convert_fusion.1 = (bf16[512,3072]{1,0:T(8,128)(2,1)S(1)}, bf16[512,3072]{1,0:T(8,128)(2,1)S(1)}, bf16[512,3072]{1,0:T(8,128)(2,1)}) fusion(f32[512,3072]{1,0:T(8,128)} %fusion.108, f32[512,3072]{1,0:T(8,128)} %fusion.109, bf16[3072,1024]{1,0:T(8,128)(2,1)} %all-gather.22.cloned.1.call-done, bf16[1,512,1024]{2,1,0:T(8,128)(2,1)} %param.36), kind=kOutput, calls=%fused_computation.70 | convolution fusion | flops 3246391296 | bytes 29360128 | tf_op jit(solution)/shard_map/td,fd->tf/dot_general | solution.py:166
  299.5 8.2 fusion.110
  307.8 3.9 multiply_reduce_fusion.4
  314.7 3.8 convolution_convert_fusion.5
  318.5 3.2 reshape.420
  323.6 144.7 %while.40 = (s32[]{:T(128)}, f32[8,2,512,128]{3,2,1,0:T(8,128)}, f32[8,1024,128]{1,2,0:T(8,128)}, f32[8,1024,128]{1,2,0:T(8,128)}, bf16[8,2,512,128]{3,2,1,0:T(8...) while((s32[]{:T(128)}, f32[8,2,512,128]{3,2,1,0:T(8,128)}, ...), condition=%wide.region_11.12_spmd.clone, body=%wide.region_9.11_spmd.clone.sunk | while | flops 1359739904 | bytes 55880860 | solution.py:218
  326.3 3.0 multiply_reduce_fusion.11
  337.7 4.3 fusion.182
  355.8 4.3 fusion.182
  373.9 4.3 fusion.182
  391.9 4.3 fusion.182
  409.9 4.4 fusion.182
  416.5 3.0 multiply_reduce_fusion.11
  427.9 4.3 fusion.182
  445.9 4.3 fusion.182
  464.0 4.4 fusion.182
  471.4 3.3 collective-permute-done.2
  486.9 14.4 %collective-permute-done.3 = bf16[512,1024]{0,1:T(8,128)(2,1)S(1)} collective-permute-done((bf16[512,1024]{0,1:T(8,128)(2,1)S(1)}, bf16[512,1024]{0,1:T(8,128)(2,1)S(1)}, u32[]{:S(2)}, u32[]{:S(2)}) %collective-permute-start.3) | collective-permute-done | bytes 1048608 | tf_op jit(solution)/shard_map/ppermute | solution.py:14
  506.7 5.3 copy.64
  512.0 3.3 multiply_add_fusion.1
  520.1 4.7 convolution_convert_fusion.4
  524.9 6.6 convolution_convert_fusion.3
  531.8 8.4 convolution_convert_fusion.2
  540.3 8.3 convolution_convert_fusion.1
  548.6 8.3 convolution_convert_fusion
  557.3 3.6 reduce-scatter.12.cloned.1.call-done
  560.9 46.9 %reduce-scatter.8.cloned.1.call-done = bf16[256,2048]{1,0:T(8,128)(2,1)} async-done(((bf16[1024,2048]{1,0:T(8,128)(2,1)}), bf16[256,2048]{1,0:T(8,128)(2,1)}) %reduce-scatter.8.cloned.1.call-update) | async-done | bytes 1048592 | tf_op jit(solution)/shard_map/reduce_scatter | solution.py:255
  607.8 47.2 %reduce-scatter.14.cloned.1.call-done = bf16[512,1024]{1,0:T(8,128)(2,1)} async-done(((bf16[2048,1024]{1,0:T(8,128)(2,1)}), bf16[512,1024]{1,0:T(8,128)(2,1)}) %reduce-scatter.14.cloned.1.call-update) | async-done | bytes 1048592 | tf_op jit(solution)/shard_map/reduce_scatter | solution.py:270
  655.1 60.8 %reduce-scatter.16.cloned.1.call-done = bf16[256,3072]{1,0:T(8,128)(2,1)} async-done(((bf16[1024,3072]{1,0:T(8,128)(2,1)}), bf16[256,3072]{1,0:T(8,128)(2,1)}) %reduce-scatter.16.cloned.1.call-update) | async-done | bytes 1572880 | tf_op jit(solution)/shard_map/reduce_scatter | solution.py:276
  715.9 61.1 %reduce-scatter.18.cloned.1.call-done = bf16[256,3072]{1,0:T(8,128)(2,1)} async-done(((bf16[1024,3072]{1,0:T(8,128)(2,1)}), bf16[256,3072]{1,0:T(8,128)(2,1)}) %reduce-scatter.18.cloned.1.call-update) | async-done | bytes 1572880 | tf_op jit(solution)/shard_map/reduce_scatter | solution.py:279
  777.0 60.8 %reduce-scatter.20.cloned.1.call-done = bf16[768,1024]{1,0:T(8,128)(2,1)} async-done(((bf16[3072,1024]{1,0:T(8,128)(2,1)}), bf16[768,1024]{1,0:T(8,128)(2,1)}) %reduce-scatter.20.cloned.1.call-update) | async-done | bytes 1572880 | tf_op jit(solution)/shard_map/reduce_scatter | solution.py:282
  839.1 5.3 fusion.111
  844.5 7.3 fusion.82
  857.0 6.1 all-reduce.13
  863.5 22.8 %all-reduce.11 = (bf16[256]{0:T(256)(128)(2,1)S(1)}, bf16[32]{0:T(256)(128)(2,1)S(1)}, bf16[32]{0:T(256)(128)(2,1)S(1)}, bf16[256]{0:T(256)(128)(2,1)S(1)}) all-reduce(bf16[256]{0:T(256)(128)(2,1)S(1)} %dynamic-slice.23, bf16[32]{0:T(256)(128)(2,1)S(1)} %dynamic-slice.25, ...), channel_id=1, replica_groups=mesh['rep'=8,'fsdp'=4] {'rep'}, use_global_device_ids=true, to_apply=%region_17.18 | all-reduce | flops 576 | bytes 2304 | tf_op jit(solution)/shard_map/psum | solution.py:288
  888.5 3.4 fusion.80
  891.9 211.8 %all-reduce.17.cloned.1.call-done = (bf16[256,2048]{1,0:T(8,128)(2,1)}, bf16[256,1024]{1,0:T(8,128)(2,1)}, bf16[256,1024]{1,0:T(8,128)(2,1)}, bf16[512,1024]{1,0...) async-done(((bf16[256,2048]{1,0:T(8,128)(2,1)}, bf16[256,1024]{1,0:T(8,128)(2,1)}, bf16[256,1024]{1,0:T(8,128)(2,1)}, ...) | async-done | bytes 7864336 | tf_op jit(solution)/shard_map/psum | solution.py:288
  1103.7 3.6 convert_element_type.281
  (347 shorter events, 213.5 us)
Async XLA Ops:
  7.2 27.9 %all-gather.12.cloned.1.call-start = ((), (), s32[]{:S(2)}) async-start(), calls=%async_computation.8 | async-start | bytes 2621440 | tf_op jit(solution)/shard_map/all_gather | solution.py:63
  7.9 52.3 %all-gather.14.cloned.1.call-start = ((), (), s32[]{:S(2)}) async-start(), calls=%async_computation.9 | async-start | bytes 2621440 | tf_op jit(solution)/shard_map/all_gather | solution.py:64
  8.7 95.7 %all-gather.10.cloned.1.call-start = ((), (), s32[]{:S(2)}) async-start(), calls=%async_computation.7 | async-start | bytes 5242880 | tf_op jit(solution)/shard_map/all_gather | solution.py:62
  9.4 7.9 copy-start.50
  9.4 9.1 copy-start.54
  9.4 9.4 copy-start.55
  9.4 17.7 %copy-start.5 = (bf16[1,512,1024]{2,1,0:T(8,128)(2,1)S(1)}, bf16[1,512,1024]{2,1,0:T(8,128)(2,1)}, u32[]{:S(2)}) copy-start(bf16[1,512,1024]{2,1,0:T(8,128)(2,1)} %param.34) | copy-start | bytes 3145732
  9.5 175.2 %all-gather.16.cloned.1.call-start = ((), (), s32[]{:S(2)}) async-start(), calls=%async_computation.10 | async-start | bytes 5242880 | tf_op jit(solution)/shard_map/all_gather | solution.py:67
  10.0 181.9 %all-gather.18.cloned.1.call-start = ((), (), s32[]{:S(2)}) async-start(), calls=%async_computation.11 | async-start | bytes 7864320 | tf_op jit(solution)/shard_map/all_gather | solution.py:69
  10.6 229.1 %all-gather.20.cloned.1.call-start = ((), (), s32[]{:S(2)}) async-start(), calls=%async_computation.12 | async-start | bytes 7864320 | tf_op jit(solution)/shard_map/all_gather | solution.py:70
  11.2 276.5 %all-gather.22.cloned.1.call-start = ((), (), s32[]{:S(2)}) async-start(), calls=%async_computation.13 | async-start | bytes 7864320 | tf_op jit(solution)/shard_map/all_gather | solution.py:71
  17.3 93.5 %copy-start.39 = (f32[4,1,256]{2,1,0:T(1,128)}, f32[4,1,256]{2,1,0:T(1,128)S(1)}, u32[]{:S(2)}) copy-start(f32[4,1,256]{2,1,0:T(1,128)S(1)} %convert_element_type.287) | copy-start | bytes 12292
  27.2 15.4 %copy-start.46 = (f32[128]{0:T(128)}, f32[128]{0:T(128)S(1)}, u32[]{:S(2)}) copy-start(f32[128]{0:T(128)S(1)} %convert_element_type.237) | copy-start | bytes 1540
  27.5 11.5 %copy-start.43 = (f32[512]{0:T(512)}, f32[512]{0:T(512)S(1)}, u32[]{:S(2)}) copy-start(f32[512]{0:T(512)S(1)} %fusion.73) | copy-start | bytes 6148
  27.5 83.3 %copy-start.41 = (f32[512]{0:T(512)}, f32[512]{0:T(512)S(1)}, u32[]{:S(2)}) copy-start(f32[512]{0:T(512)S(1)} %fusion.100) | copy-start | bytes 6148
  28.0 88.3 %copy-start.13 = (f32[512,64]{0,1:T(8,128)}, f32[512,64]{0,1:T(8,128)S(1)}, u32[]{:S(2)}) copy-start(f32[512,64]{0,1:T(8,128)S(1)} %get-tuple-element.496) | copy-start | bytes 393220
  28.1 88.3 %copy-start.15 = (f32[512,64]{0,1:T(8,128)}, f32[512,64]{0,1:T(8,128)S(1)}, u32[]{:S(2)}) copy-start(f32[512,64]{0,1:T(8,128)S(1)} %get-tuple-element.497) | copy-start | bytes 393220
  43.8 20.3 %copy-start.10 = (bf16[512,8,128]{0,2,1:T(8,128)(2,1)}, bf16[512,8,128]{0,2,1:T(8,128)(2,1)S(1)}, u32[]{:S(2)}) copy-start(bf16[512,8,128]{0,2,1:T(8,128)(2,1)S(1)} %maximum_convert_fusion) | copy-start | bytes 3145732
  43.8 23.2 %copy-start.45 = (s32[1,2048]{1,0:T(1,128)S(1)}, s32[1,2048]{1,0:T(1,128)}, u32[]{:S(2)}) copy-start(s32[1,2048]{1,0:T(1,128)} %param.35) | copy-start | bytes 24580
  43.8 23.3 %copy-start.56 = (bf16[256]{0:T(256)(128)(2,1)S(1)}, bf16[256]{0:T(256)(128)(2,1)}, u32[]{:S(2)}) copy-start(bf16[256]{0:T(256)(128)(2,1)} %param.44) | copy-start | bytes 1540
  43.8 30.1 %collective-permute-start = (bf16[512,1024]{0,1:T(8,128)(2,1)S(1)}, bf16[512,1024]{0,1:T(8,128)(2,1)S(1)}, u32[]{:S(2)}, u32[]{:S(2)}) collective-permute-start(bf16[512,1024]{0,1:T(8,128)(2,1)S(1)} %bitcast.251), channel_id=1, source_target_pairs={{0,1},{1,2},{2,3},{4,5},{5,6},{6,7},{8,9},{9,10},{10,11},{12,13},{... | collective-permute-start | bytes 3145736 | tf_op jit(solution)/shard_map/ppermute | solution.py:14
  64.1 15.3 %collective-permute-start.1 = (bf16[512,1024]{1,0:T(8,128)(2,1)}, bf16[512,1024]{1,0:T(8,128)(2,1)}, u32[]{:S(2)}, u32[]{:S(2)}) collective-permute-start(bf16[512,1024]{1,0:T(8,128)(2,1)} %convolution_convert_fusion.8), channel_id=1, source_target_pairs={{0,1},{1,2},{2,3},{4,5},{5,6},{6,7},{8,9},{9,10},{10,11},{12,13},{... | collective-permute-start | bytes 3145736 | tf_op jit(solution)/shard_map/ppermute | solution.py:14
  66.9 490.4 %reduce-scatter.10.cloned.1.call-start = ((), (), s32[]{:S(2)}) async-start(), calls=%async_computation.15 | async-start | bytes 2621440 | tf_op jit(solution)/shard_map/reduce_scatter | solution.py:258
  67.0 48.5 %copy-start.48 = (f32[128]{0:T(128)}, f32[128]{0:T(128)S(1)}, u32[]{:S(2)}) copy-start(f32[128]{0:T(128)S(1)} %convert_element_type.235) | copy-start | bytes 1540
  115.5 2.1 copy-start.1
  115.5 2.1 copy-start.35
  115.5 2.0 copy-start.29
  189.9 121.9 %copy-start.7 = (f32[512,1024]{1,0:T(8,128)}, f32[512,1024]{1,0:T(8,128)S(1)}, u32[]{:S(2)}) copy-start(f32[512,1024]{1,0:T(8,128)S(1)} %get-tuple-element.505) | copy-start | bytes 6291460
  190.2 49.6 %copy-start.24 = (bf16[512,1024]{1,0:T(8,128)(2,1)}, bf16[512,1024]{1,0:T(8,128)(2,1)S(1)}, u32[]{:S(2)}) copy-start(bf16[512,1024]{1,0:T(8,128)(2,1)S(1)} %multiply_convert_fusion.3) | copy-start | bytes 3145732
  299.5 8.2 copy-start.58
  299.5 8.2 copy-start.57
  299.5 8.3 copy-start.51
  307.8 4.0 copy-start.25
  311.8 2.9 copy-start.52
  325.8 3.5 copy-start
  343.8 3.5 copy-start
  361.9 3.5 copy-start
  379.9 3.5 copy-start
  397.9 3.5 copy-start
  416.0 3.5 copy-start
  434.0 3.5 copy-start
  452.0 3.5 copy-start
  470.1 4.6 collective-permute-start.2
  474.6 2.0 copy-start.16
  483.7 77.2 %reduce-scatter.12.cloned.1.call-start = ((), (), s32[]{:S(2)}) async-start(), calls=%async_computation.16 | async-start | bytes 2621440 | tf_op jit(solution)/shard_map/reduce_scatter | solution.py:261
  485.4 15.9 %collective-permute-start.3 = (bf16[512,1024]{0,1:T(8,128)(2,1)S(1)}, bf16[512,1024]{0,1:T(8,128)(2,1)S(1)}, u32[]{:S(2)}, u32[]{:S(2)}) collective-permute-start(bf16[512,1024]{0,1:T(8,128)(2,1)S(1)} %bitcast.263), channel_id=1, source_target_pairs={{1,0},{2,1},{3,2},{5,4},{6,5},{7,6},{9,8},{10,9},{11,10},{13,12},{... | collective-permute-start | bytes 3145736 | tf_op jit(solution)/shard_map/ppermute | solution.py:14
  501.3 2.5 copy-start.11
  506.7 101.2 %reduce-scatter.8.cloned.1.call-start = ((), (), s32[]{:S(2)}) async-start(), calls=%async_computation.14 | async-start | bytes 5242880 | tf_op jit(solution)/shard_map/reduce_scatter | solution.py:255
  512.0 3.5 copy-start.2
  512.0 3.5 copy-start.30
  512.0 3.5 copy-start.49
  524.9 130.2 %reduce-scatter.14.cloned.1.call-start = ((), (), s32[]{:S(2)}) async-start(), calls=%async_computation.17 | async-start | bytes 5242880 | tf_op jit(solution)/shard_map/reduce_scatter | solution.py:270
  531.5 184.3 %reduce-scatter.16.cloned.1.call-start = ((), (), s32[]{:S(2)}) async-start(), calls=%async_computation.18 | async-start | bytes 7864320 | tf_op jit(solution)/shard_map/reduce_scatter | solution.py:276
  540.2 236.8 %reduce-scatter.18.cloned.1.call-start = ((), (), s32[]{:S(2)}) async-start(), calls=%async_computation.19 | async-start | bytes 7864320 | tf_op jit(solution)/shard_map/reduce_scatter | solution.py:279
  548.6 289.2 %reduce-scatter.20.cloned.1.call-start = ((), (), s32[]{:S(2)}) async-start(), calls=%async_computation.20 | async-start | bytes 7864320 | tf_op jit(solution)/shard_map/reduce_scatter | solution.py:282
  557.0 546.8 %all-reduce.17.cloned.1.call-start = ((), (), s32[]{:S(2)}) async-start(), calls=%async_computation.21 | async-start | bytes 15728640 | tf_op jit(solution)/shard_map/psum | solution.py:288
  839.1 5.4 copy-start.8
  839.1 5.4 copy-start.59
  844.5 7.3 copy-start.12
  855.2 33.3 %copy-start.44 = (f32[512]{0:T(512)S(1)}, f32[512]{0:T(512)}, u32[]{:S(2)}) copy-start(f32[512]{0:T(512)} %copy-done.43) | copy-start | bytes 6148
  1103.7 3.6 copy-start.21
  1107.3 2.0 copy-start.20
  1109.3 2.1 copy-start.23
  1113.0 2.7 copy-start.31
  (22 other events, 31.9 us)
Sparse Core Ops, SparseCore 0:
  9.6 25.4 all-gather.11
  36.6 23.5 all-gather.13
  61.8 42.5 all-gather.9
  105.8 38.1 all-gather.15
  145.5 46.4 all-gather.17
  193.3 46.3 all-gather.19
  241.3 46.3 all-gather.21
  483.8 42.9 reduce-scatter.9
  529.4 31.4 reduce-scatter.11
  563.3 44.4 reduce-scatter.7
  610.5 44.5 reduce-scatter.13
  657.5 58.3 reduce-scatter.15
  718.6 58.3 reduce-scatter.17
  779.4 58.3 reduce-scatter.19
  843.9 259.8 all-reduce.16
where the time goes:
time: 1130 us; the launch traced here: 1120 us
  waiting for transfers between devices  638 us (56%)
  matrix products  274 us (24%)
  other arithmetic  74 us (7%)
  local copies, waits for them, and re-layouts  61.2 us (5%)
  blocking collectives  49.9 us (4%)
  between operations  17.2 us (2%)
    psum x1, waiting for transfers between devices, body(): lax.psum(shortened(tuple(owned)), 'rep')  212 us
    reduce_scatter x1, waiting for transfers between devices, body(): lax.psum_scatter(upper_grad.astype(jnp.bfloat16), 'fsdp', scatter_dimensi...  61.1 us
    reduce_scatter x1, waiting for transfers between devices, body(): lax.psum_scatter(gate_grad.astype(jnp.bfloat16), 'fsdp', scatter_dimensio...  60.8 us
    reduce_scatter x1, waiting for transfers between devices, body(): lax.psum_scatter(down_grad.astype(jnp.bfloat16), 'fsdp', scatter_dimensio...  60.8 us
    reduce_scatter x1, waiting for transfers between devices, body(): lax.psum_scatter(out_grad.astype(jnp.bfloat16), 'fsdp', scatter_dimension...  47.2 us
    reduce_scatter x1, waiting for transfers between devices, body(): lax.psum_scatter(wquery_grad.astype(jnp.bfloat16), 'fsdp', scatter_dimens...  46.9 us
    all_gather x1, waiting for transfers between devices, body(): lax.all_gather(down_weight, 'fsdp', axis=0, tiled=True)  39.9 us
    all_gather x1, waiting for transfers between devices, body(): lax.all_gather(up_weight, 'fsdp', axis=0, tiled=True)  39.5 us
  transfers between devices with their start and end apart: 19, of which 15 were waited for; matrix products, arithmetic and copies ran while one was open for 18% of the time, Pallas kernels for 0%

commit v1 on v0

v1 whole, which is shorter than its diff:
```python
import functools

import jax
import jax.numpy as jnp
from jax import lax
from jax.experimental import pallas as pl
from jax.experimental.pallas import tpu as pltpu
from jax.sharding import PartitionSpec as P

EPSILON = 1e-06
ROPE_BASE = 1000000.0
MASKED = -1e30
LOG2E = 1.4426950408889634
BF = jnp.bfloat16
F32 = jnp.float32


def mm(a, b, ca=1, cb=0):
    return lax.dot_general(a, b, (((ca,), (cb,)), ((), ())), preferred_element_type=F32)


def flip(value, axis, bit):
    count = lax.axis_size(axis)
    return lax.ppermute(value, axis, [(i, i ^ bit) for i in range(count)])


def own_bit(axis, bit):
    return (lax.axis_index(axis) // bit) % 2


def bits_of(axis):
    count, bits, bit = lax.axis_size(axis), [], 1
    while bit < count:
        bits.append(bit)
        bit *= 2
    return bits


def pair(mine, theirs, upper, axis):
    low = jnp.where(upper, theirs, mine)
    high = jnp.where(upper, mine, theirs)
    return jnp.stack([low, high], axis=axis)


def gather(shard):
    block = shard
    for depth, bit in enumerate(reversed(bits_of("fsdp"))):
        block = pair(block, flip(block, "fsdp", bit), own_bit("fsdp", bit) == 1, depth)
    return block.reshape((-1,) + shard.shape[1:])


def half(blocks, axis, which):
    return lax.dynamic_index_in_dim(blocks, which, axis, keepdims=False)


def scatter_product(rows, cols):
    tokens, width = rows.shape
    count = lax.axis_size("fsdp")
    bits = bits_of("fsdp")
    own = width // count
    mine = own_bit("fsdp", 1)
    split = rows.reshape(tokens, count // 2, 2, own)
    sent = half(split, 2, 1 - mine).reshape(tokens, width // 2)
    kept = half(split, 2, mine).reshape(tokens, width // 2)
    arrived = flip(mm(sent, cols, 0, 0).astype(BF), "fsdp", 1)
    part = (mm(kept, cols, 0, 0) + arrived.astype(F32)).astype(BF)
    for bit in bits[1:]:
        mine = own_bit("fsdp", bit)
        remaining = part.shape[0] // own
        view = part.reshape(remaining // 2, 2, own, -1)
        arrived = flip(half(view, 1, 1 - mine), "fsdp", bit)
        part = (half(view, 1, mine).astype(F32) + arrived.astype(F32)).astype(BF)
        part = part.reshape((remaining // 2) * own, -1)
    return part


def sum_rep(part):
    bits = bits_of("rep")
    shape = part.shape
    for bit in bits:
        mine = own_bit("rep", bit)
        view = part.reshape(2, part.shape[0] // 2, shape[1])
        arrived = flip(half(view, 0, 1 - mine), "rep", bit)
        total = half(view, 0, mine).astype(F32) + arrived.astype(F32)
        part = total.astype(BF)
    for bit in reversed(bits):
        block = pair(part, flip(part, "rep", bit), own_bit("rep", bit) == 1, 0)
        part = block.reshape(-1, shape[1])
    return part.astype(F32)


def sum_all(vector):
    for axis in ("fsdp", "rep"):
        for bit in bits_of(axis):
            vector = vector + flip(vector, axis, bit)
    return vector


def passed_along(value, axis, steps):
    count = lax.axis_size(axis)
    first, last = (max(0, -steps), min(count, count - steps))
    return lax.ppermute(value, axis, [(source, source + steps) for source in range(first, last)])


def rms_scale(field, scaling):
    return field * lax.rsqrt(jnp.mean(field * field, axis=-1, keepdims=True) + EPSILON) * scaling


def rope_tables(positions, head_width):
    freqs = ROPE_BASE ** (-(jnp.arange(head_width // 2, dtype=F32) * 2.0 / head_width))
    angle_table = positions[:, None] * freqs[None, :]
    cosine, sine = jnp.cos(angle_table), jnp.sin(angle_table)
    return (
        jnp.concatenate([cosine, cosine], axis=1),
        jnp.concatenate([-sine, sine], axis=1),
    )


def swap(field):
    return pltpu.roll(field, field.shape[-1] // 2, 1)


def turn(raw, gain, cosine, sine):
    scaled = rms_scale(raw, gain)
    return scaled * cosine + swap(scaled) * sine


def turn_back(raw, gain, cosine, sine, grad):
    inverse = lax.rsqrt(jnp.mean(raw * raw, axis=-1, keepdims=True) + EPSILON)
    unit = raw * inverse
    grad = grad * cosine + swap(grad * sine)
    gain_part = jnp.sum(grad * unit, axis=0, keepdims=True)
    grad = grad * gain
    back = inverse * (grad - unit * jnp.mean(grad * unit, axis=-1, keepdims=True))
    return back, gain_part


def full_spec(shape):
    return pl.BlockSpec(shape, lambda h: (0, 0))


def head_spec(rows, width):
    return pl.BlockSpec((rows, width), lambda h: (0, h))


def params():
    return pltpu.CompilerParams(vmem_limit_bytes=40 * 1024 * 1024)


def turn_kernel(raw, gain, cosine, sine, out):
    out[...] = turn(raw[...], gain[...], cosine[...], sine[...]).astype(BF)


def turn_call(raw, gain, cosine, sine):
    tokens, width = raw.shape
    hd = gain.shape[1]
    return pl.pallas_call(
        turn_kernel,
        grid=(width // hd,),
        in_specs=[
            head_spec(tokens, hd),
            full_spec((1, hd)),
            full_spec((tokens, hd)),
            full_spec((tokens, hd)),
        ],
        out_specs=head_spec(tokens, hd),
        out_shape=jax.ShapeDtypeStruct((tokens, width), BF),
        compiler_params=params(),
        cost_estimate=pl.CostEstimate(
            flops=tokens * width * 10, bytes_accessed=tokens * width * 6, transcendentals=0
        ),
    )(raw, gain, cosine, sine)


def turn_back_kernel(raw, gain, cosine, sine, grad, back, gain_part):
    result, part = turn_back(raw[...], gain[...], cosine[...], sine[...], grad[...])
    back[...] = result.astype(BF)

    @pl.when(pl.program_id(0) == 0)
    def _():
        gain_part[...] = jnp.zeros_like(gain_part)

    gain_part[...] += part


def turn_back_call(raw, gain, cosine, sine, grad):
    tokens, width = raw.shape
    hd = gain.shape[1]
    return pl.pallas_call(
        turn_back_kernel,
        grid=(width // hd,),
        in_specs=[
            head_spec(tokens, hd),
            full_spec((1, hd)),
            full_spec((tokens, hd)),
            full_spec((tokens, hd)),
            head_spec(tokens, hd),
        ],
        out_specs=[head_spec(tokens, hd), full_spec((1, hd))],
        out_shape=[
            jax.ShapeDtypeStruct((tokens, width), BF),
            jax.ShapeDtypeStruct((1, hd), F32),
        ],
        compiler_params=params(),
        cost_estimate=pl.CostEstimate(
            flops=tokens * width * 20, bytes_accessed=tokens * width * 10, transcendentals=0
        ),
    )(raw, gain, cosine, sine, grad)


def tile_bias(seg_query, seg_keys, at, rows, span):
    shape = (rows, span + rows)
    q = lax.broadcasted_iota(jnp.int32, shape, 0)
    k = lax.broadcasted_iota(jnp.int32, shape, 1)
    same = seg_query[pl.ds(at, rows), :] == seg_keys[:, pl.ds(at, span + rows)]
    return jnp.where(same & (k - span <= q), 0.0, MASKED).astype(F32)


def window(tail, own, at, rows):
    return jnp.concatenate([tail[at:, :], own[0 : at + rows, :]], axis=0)


def attend_kernel(rows, q, kt, k, vt, v, segq, segk, out, bias):
    tokens, hd = kt.shape
    scale = hd ** (-0.5) * LOG2E
    tiles = tokens // rows

    @pl.when(pl.program_id(0) == 0)
    def _():
        for i in range(tiles):
            bias[i] = tile_bias(segq, segk, i * rows, rows, tokens)

    for i in range(tiles):
        at = i * rows
        keys = window(kt, k, at, rows)
        values = window(vt, v, at, rows)
        for g in range(q.shape[1] // hd):
            cols = slice(g * hd, (g + 1) * hd)
            s = mm(q[at : at + rows, cols], keys, 1, 1) * scale + bias[i]
            e = jnp.exp2(s)
            inverse = 1.0 / jnp.sum(e, axis=1, keepdims=True)
            p = (e * inverse).astype(BF)
            out[at : at + rows, cols] = mm(p, values).astype(BF)


def attend_call(q, kt, k, vt, v, segq, segk, hd, rows):
    tokens, width = q.shape
    kvh = k.shape[1] // hd
    gw = width // kvh
    return pl.pallas_call(
        functools.partial(attend_kernel, rows),
        grid=(kvh,),
        in_specs=[head_spec(tokens, gw)]
        + [head_spec(tokens, hd)] * 4
        + [full_spec((tokens, 1)), full_spec((1, 2 * tokens))],
        out_specs=head_spec(tokens, gw),
        out_shape=jax.ShapeDtypeStruct((tokens, width), BF),
        scratch_shapes=[pltpu.VMEM((tokens // rows, rows, tokens + rows), F32)],
        compiler_params=params(),
        cost_estimate=pl.CostEstimate(
            flops=4 * tokens * 2 * tokens * width * 3,
            bytes_accessed=tokens * width * 8,
            transcendentals=0,
        ),
    )(q, kt, k, vt, v, segq, segk)


def attend_back_kernel(
    rows, q, kt, k, vt, v, do, raw, gain, cosine, sine, segq, segk,
    back, gain_part, dkt, dk, dvt, dv, bias, dkw, dvw,
):
    tokens, hd = kt.shape
    scale = hd ** (-0.5)
    tiles = tokens // rows
    first = pl.program_id(0) == 0

    @pl.when(first)
    def _():
        gain_part[...] = jnp.zeros_like(gain_part)
        for i in range(tiles):
            bias[i] = tile_bias(segq, segk, i * rows, rows, tokens)

    dkw[...] = jnp.zeros_like(dkw)
    dvw[...] = jnp.zeros_like(dvw)
    for i in range(tiles):
        at = i * rows
        keys = window(kt, k, at, rows)
        values = window(vt, v, at, rows)
        band = slice(at, at + tokens + rows)
        here = slice(at, at + rows)
        for g in range(q.shape[1] // hd):
            cols = slice(g * hd, (g + 1) * hd)
            qt = q[here, cols]
            dot = do[here, cols]
            e = jnp.exp2(mm(qt, keys, 1, 1) * (scale * LOG2E) + bias[i])
            p = e * (1.0 / jnp.sum(e, axis=1, keepdims=True))
            dp = mm(dot, values, 1, 1)
            dvw[band, :] += mm(p.astype(BF), dot, 0, 0)
            centre = jnp.sum(dp * p, axis=1, keepdims=True)
            ds = (p * (dp - centre)).astype(BF)
            dkw[band, :] += mm(ds, qt, 0, 0)
            dq = mm(ds, keys) * scale
            result, part = turn_back(
                raw[here, cols], gain[...], cosine[here, :], sine[here, :], dq
            )
            back[here, cols] = result.astype(BF)
            gain_part[...] += part
    dkt[...] = (dkw[0:tokens, :] * scale).astype(BF)
    dk[...] = dkw[tokens:, :] * scale
    dvt[...] = dvw[0:tokens, :].astype(BF)
    dv[...] = dvw[tokens:, :]


def attend_back_call(q, kt, k, vt, v, do, raw, gain, cosine, sine, segq, segk, hd, rows, start, count):
    tokens, width = q.shape
    kvh = k.shape[1] // hd
    gw = width // kvh

    def shifted(block):
        return pl.BlockSpec((tokens, block), lambda h: (0, h + start))

    kv = jax.ShapeDtypeStruct((tokens, count * hd), F32)
    kv_sent = jax.ShapeDtypeStruct((tokens, count * hd), BF)
    return pl.pallas_call(
        functools.partial(attend_back_kernel, rows),
        grid=(count,),
        in_specs=[shifted(gw)]
        + [shifted(hd)] * 4
        + [
            shifted(gw),
            shifted(gw),
            full_spec((1, hd)),
            full_spec((tokens, hd)),
            full_spec((tokens, hd)),
            full_spec((tokens, 1)),
            full_spec((1, 2 * tokens)),
        ],
        out_specs=[head_spec(tokens, gw), full_spec((1, hd))] + [head_spec(tokens, hd)] * 4,
        out_shape=[
            jax.ShapeDtypeStruct((tokens, count * gw), BF),
            jax.ShapeDtypeStruct((1, hd), F32),
            kv_sent,
            kv,
            kv_sent,
            kv,
        ],
        scratch_shapes=[
            pltpu.VMEM((tokens // rows, rows, tokens + rows), F32),
            pltpu.VMEM((2 * tokens, hd), F32),
            pltpu.VMEM((2 * tokens, hd), F32),
        ],
        compiler_params=params(),
        cost_estimate=pl.CostEstimate(
            flops=10 * tokens * 2 * tokens * count * gw * 2,
            bytes_accessed=tokens * count * gw * 20,
            transcendentals=0,
        ),
    )(q, kt, k, vt, v, do, raw, gain, cosine, sine, segq, segk)


def gating(gate, upper):
    return jax.nn.silu(gate) * upper


def body(
    tokens,
    segments,
    cotangent,
    attn_gain,
    query_weight,
    key_weight,
    value_weight,
    query_gain,
    key_gain,
    out_weight,
    mlp_gain,
    gate_weight,
    up_weight,
    down_weight,
):
    gains = [attn_gain, mlp_gain, query_gain, key_gain]
    packed = gather(jnp.concatenate(gains)[None, :])
    wkey, wvalue, wquery = gather(key_weight), gather(value_weight), gather(query_weight)
    wout, wgate, wupper, wdown = (
        gather(out_weight),
        gather(gate_weight),
        gather(up_weight),
        gather(down_weight),
    )
    whole, at = [], 0
    for item in gains:
        whole.append(packed[:, at : at + item.shape[0]].reshape(-1).astype(F32))
        at += item.shape[0]
    attn_full, mlp_full, qgain, kgain = whole
    qgain, kgain = qgain[None, :], kgain[None, :]
    tok_rows = tokens.shape[1]
    hd = qgain.shape[1]
    kvh = wkey.shape[1] // hd
    rows = min(256, tok_rows)
    place = lax.axis_index("fsdp")
    inputs = tokens[0].astype(F32)
    positions = (place * tok_rows + jnp.arange(tok_rows, dtype=jnp.int32)).astype(F32)
    cosine, sine = rope_tables(positions, hd)
    padded_seg = jnp.concatenate([jnp.full((tok_rows,), -1, jnp.int32), segments[0]])
    window_seg = lax.dynamic_slice_in_dim(padded_seg, place * tok_rows, 2 * tok_rows)
    segk = window_seg[None, :]
    segq = window_seg[tok_rows:, None]
    normed, pull_attn = jax.vjp(rms_scale, inputs, attn_full)
    act = normed.astype(BF)
    key_raw = mm(act, wkey)
    value = mm(act, wvalue).astype(BF)
    key = turn_call(key_raw, kgain, cosine, sine)
    key_tail, value_tail = passed_along(key, "fsdp", 1), passed_along(value, "fsdp", 1)
    query_raw = mm(act, wquery)
    query = turn_call(query_raw, qgain, cosine, sine)
    mixed = attend_call(query, key_tail, key, value_tail, value, segq, segk, hd, rows)
    hidden = inputs + mm(mixed, wout)
    normed2, pull_mlp = jax.vjp(rms_scale, hidden, mlp_full)
    act2 = normed2.astype(BF)
    gate = mm(act2, wgate)
    upper = mm(act2, wupper)
    inner_f, pull_gate = jax.vjp(gating, gate, upper)
    inner = inner_f.astype(BF)
    grad_out = cotangent[0]
    down_part = scatter_product(inner, grad_out)
    final = (hidden + mm(inner, wdown)).astype(BF)
    inner_grad = mm(grad_out, wdown, 1, 1)
    gate_back, upper_back = pull_gate(inner_grad)
    gate_back = gate_back.astype(BF)
    upper_back = upper_back.astype(BF)
    gate_part = scatter_product(act2, gate_back)
    upper_part = scatter_product(act2, upper_back)
    act2_grad = mm(gate_back, wgate, 1, 1) + mm(upper_back, wupper, 1, 1)
    hidden_norm_grad, mlp_gain_part = pull_mlp(act2_grad)
    hidden_grad = grad_out.astype(F32) + hidden_norm_grad
    branch_grad = hidden_grad.astype(BF)
    out_part = scatter_product(mixed, branch_grad)
    mixed_grad = mm(branch_grad, wout, 1, 1).astype(BF)
    groups = 2 if kvh % 2 == 0 else 1
    count = kvh // groups
    gw = query.shape[1] // kvh
    query_gain_part = jnp.zeros((1, hd), F32)
    key_gain_part = jnp.zeros((1, hd), F32)
    act_grad = None
    qkv_parts = []
    for n in range(groups):
        query_back, qpart, dkt, dk, dvt, dv = attend_back_call(
            query, key_tail, key, value_tail, value, mixed_grad, query_raw, qgain,
            cosine, sine, segq, segk, hd, rows, n * count, count,
        )
        own = slice(n * count * hd, (n + 1) * count * hd)
        key_own = dk + passed_along(dkt, "fsdp", -1).astype(F32)
        value_back = (dv + passed_along(dvt, "fsdp", -1).astype(F32)).astype(BF)
        key_back, kpart = turn_back_call(key_raw[:, own], kgain, cosine, sine, key_own)
        query_gain_part = query_gain_part + qpart
        key_gain_part = key_gain_part + kpart
        together = jnp.concatenate([query_back, key_back, value_back], axis=1)
        qkv_parts.append(scatter_product(act, together))
        wide = slice(n * count * gw, (n + 1) * count * gw)
        term = (
            mm(query_back, wquery[:, wide], 1, 1)
            + mm(key_back, wkey[:, own], 1, 1)
            + mm(value_back, wvalue[:, own], 1, 1)
        )
        act_grad = term if act_grad is None else act_grad + term
    input_norm_grad, attn_gain_part = pull_attn(act_grad)
    inputs_grad = hidden_grad + input_norm_grad
    down_sum, gate_sum, upper_sum, out_sum = (
        sum_rep(down_part),
        sum_rep(gate_part),
        sum_rep(upper_part),
        sum_rep(out_part),
    )
    qkv_sums = [sum_rep(part) for part in qkv_parts]
    nq, nk = count * gw, count * hd
    query_sum = jnp.concatenate([s[:, :nq] for s in qkv_sums], axis=1)
    key_sum = jnp.concatenate([s[:, nq : nq + nk] for s in qkv_sums], axis=1)
    value_sum = jnp.concatenate([s[:, nq + nk :] for s in qkv_sums], axis=1)
    vector = jnp.concatenate(
        [attn_gain_part, mlp_gain_part, query_gain_part[0], key_gain_part[0]]
    )
    vector = sum_all(vector)
    parts, at = [], 0
    for item in gains:
        width = item.shape[0]
        parts.append(lax.dynamic_slice_in_dim(vector, at + place * width, width))
        at += width * lax.axis_size("fsdp")
    return (
        final[None],
        inputs_grad[None],
        parts[0],
        query_sum,
        key_sum,
        value_sum,
        parts[2],
        parts[3],
        out_sum,
        parts[1],
        gate_sum,
        upper_sum,
        down_sum,
    )


def solution(mesh):
    in_specs = (
        P("rep", "fsdp", None),
        P("rep", None),
        P("rep", "fsdp", None),
        P("fsdp"),
        P("fsdp", None),
        P("fsdp", None),
        P("fsdp", None),
        P("fsdp"),
        P("fsdp"),
        P("fsdp", None),
        P("fsdp"),
        P("fsdp", None),
        P("fsdp", None),
        P("fsdp", None),
    )
    out_specs = (
        P("rep", "fsdp", None),
        P("rep", "fsdp", None),
        P("fsdp"),
        P("fsdp", None),
        P("fsdp", None),
        P("fsdp", None),
        P("fsdp"),
        P("fsdp"),
        P("fsdp", None),
        P("fsdp"),
        P("fsdp", None),
        P("fsdp", None),
        P("fsdp", None),
    )
    return jax.shard_map(body, mesh=mesh, in_specs=in_specs, out_specs=out_specs, check_vma=False)
```

time: 1130 us -> 835 us (0.74)
  waiting for transfers between devices: 638 us -> 402 us
  matrix products: 274 us -> 101 us
  starting transfers between devices: 8.99 us -> 87 us
  Pallas kernels: 0 us -> 61.5 us
  blocking collectives: 49.9 us -> 0 us
  local copies, waits for them, and re-layouts: 61.2 us -> 107 us
  between operations: 17.2 us -> 3.23 us
    ppermute x0 -> x69, waiting for transfers between devices: none -> 402 us  [flip(): return lax.ppermute(value, axis, [(i, i ^ bit) for i in range(count)])]
    reduce_scatter x7 -> x0, waiting for transfers between devices: 280 us -> none  [the longest x1 61.1 us: body(): lax.psum_scatter(upper_grad.astype(jnp.bfloat16), 'fsdp', scatter_dimensi...]
    psum x1 -> x0, waiting for transfers between devices: 212 us -> none  [body(): lax.psum(shortened(tuple(owned)), 'rep')]
    dot_general x77 -> x29, matrix products: 274 us -> 101 us  [mm(): lax.dot_general(a, b, (((ca,), (cb,)), ((), ())), preferred_element_type=...]
    all_gather x7 -> x0, waiting for transfers between devices: 124 us -> none  [the longest x1 39.9 us: body(): lax.all_gather(down_weight, 'fsdp', axis=0, tiled=True)]
    ppermute x0 -> x69, starting transfers between devices: none -> 75.1 us  [flip(): return lax.ppermute(value, axis, [(i, i ^ bit) for i in range(count)])]
    pallas_call x0 -> x7, Pallas kernels: none -> 61.5 us  [the longest x2 35.5 us: attend_back_call(): pl.pallas_call(functools.partial(attend_back_kernel, rows), grid=(count,)...]
    unnamed x130 -> x186, local copies, waits for them, and re-layouts: 15.2 us -> 55.4 us
  transfers between devices with their start and end apart: 19 -> 75, of which waited for: 15 -> 36; matrix products, arithmetic and copies ran while one was open for 18% -> 21% of each run, Pallas kernels for 0% -> 7%
where the time goes in v1:
time: 835 us; the launch traced here: 826 us
  waiting for transfers between devices  402 us (48%)
  local copies, waits for them, and re-layouts  107 us (13%)
  matrix products  101 us (12%)
  starting transfers between devices  87 us (10%)
  other arithmetic  64.5 us (8%)
  Pallas kernels  61.5 us (7%)
    ppermute x69, waiting for transfers between devices, flip(): return lax.ppermute(value, axis, [(i, i ^ bit) for i in range(count)])  402 us
    dot_general x29, matrix products, mm(): lax.dot_general(a, b, (((ca,), (cb,)), ((), ())), preferred_element_type=...  101 us
    ppermute x69, starting transfers between devices, flip(): return lax.ppermute(value, axis, [(i, i ^ bit) for i in range(count)])  75.1 us
    unnamed x186, local copies, waits for them, and re-layouts  55.4 us
    pallas_call x2, Pallas kernels, attend_back_call(): pl.pallas_call(functools.partial(attend_back_kernel, rows), grid=(count,)...  35.5 us
    another operation x66, other arithmetic, pair(): return jnp.stack([low, high], axis=axis)  33.9 us
    dynamic_slice x4, local copies, waits for them, and re-layouts, half(): return lax.dynamic_index_in_dim(blocks, which, axis, keepdims=False)  23.9 us
  transfers between devices with their start and end apart: 75, of which 36 were waited for; matrix products, arithmetic and copies ran while one was open for 21% of the time, Pallas kernels for 7%

profile of v1, /device:TPU:0, one launch (start us, length us, event | category | flops | bytes accessed | tf_op | source)
XLA Modules:
  0.0 826.3 jit_solution(12318644617486002681)
XLA Ops:
  12.2 82.4 %collective-permute-done = bf16[1,576]{1,0:T(2,128)(2,1)S(1)} collective-permute-done((bf16[1,576]{1,0:T(2,128)(2,1)S(1)}, bf16[1,576]{1,0:T(2,128)(2,1)S(1)}, u32[]{:S(2)}, u32[]{:S(2)}) %collective-permute-start) | collective-permute-done | bytes 1184 | tf_op jit(solution)/shard_map/ppermute | solution.py:24
  98.0 4.2 copy.60
  110.9 17.4 %collective-permute-done.2 = bf16[256,2048]{1,0:T(8,128)(2,1)} collective-permute-done((bf16[256,2048]{1,0:T(8,128)(2,1)S(1)}, bf16[256,2048]{1,0:T(8,128)(2,1)}, u32[]{:S(2)}, u32[]{:S(2)}) %collective-permute-start.2) | collective-permute-done | bytes 1048608 | tf_op jit(solution)/shard_map/ppermute | solution.py:24
  129.6 21.0 %collective-permute-done.10 = bf16[512,1024]{1,0:T(8,128)(2,1)S(1)} collective-permute-done((bf16[512,1024]{1,0:T(8,128)(2,1)S(1)}, bf16[512,1024]{1,0:T(8,128)(2,1)S(1)}, u32[]{:S(2)}, u32[]{:S(2)}) %collective-permute-start.10) | collective-permute-done | bytes 1048608 | tf_op jit(solution)/shard_map/ppermute | solution.py:24
  162.5 3.9 collective-permute-start.6
  171.4 12.7 %collective-permute-done.16 = bf16[768,1024]{1,0:T(8,128)(2,1)} collective-permute-done((bf16[768,1024]{1,0:T(8,128)(2,1)}, bf16[768,1024]{1,0:T(8,128)(2,1)}, u32[]{:S(2)}, u32[]{:S(2)}) %collective-permute-start.16) | collective-permute-done | bytes 1572896 | tf_op jit(solution)/shard_map/ppermute | solution.py:24
  196.5 4.6 shard_map.237.q
  201.2 15.7 %shard_map.239 = bf16[512,2048]{1,0:T(8,128)(2,1)S(1)} custom-call(bf16[512,2048]{1,0:T(8,128)(2,1)S(1)} %shard_map.237.q, bf16[512,1024]{1,0:T(8,128)(2,1)S(1)} %collective-permute-done.6.kt, bf16[512,1024]{1,0:T(8,128)(2,1)S(1)} %shard_map.238.k, bf16[512,1024]{1,0:T(8,128)(2,1)S(1)} %collective-permute-done.9.vt, ...), custom_call_target="tpu_custom_call" | custom-call | flops 12884901888 | bytes 8388608 | tf_op jit(solution)/shard_map/pallas_call | solution.py:250
  221.5 4.5 reshape.497
  239.2 5.1 constant_dynamic-slice_fusion.2
  246.6 3.6 copy.71
  250.3 8.6 %constant_dynamic-slice_fusion.5 = (bf16[512,2,1,512]{3,2,1,0:T(2,128)(2,1)}, bf16[512,2,1,512]{3,2,1,0:T(2,128)(2,1)}) fusion(bf16[512,2,2,512]{3,2,1,0:T(2,128)(2,1)} %reshape.497, s32[]{:T(128)S(6)} %select_n.749, s32[]{:T(128)S(6)} %select_n.750), kind=kLoop, calls=%fused_computation.263 | loop fusion | bytes 4194312 | tf_op jit(solution)/shard_map/jit(dynamic_index_in_dim)/dynamic_slice | solution.py:53
  258.8 5.8 copy.70
  264.7 5.8 copy.69
  279.4 3.2 pad_maximum_fusion
  282.6 5.4 fusion.92
  290.7 7.6 fusion.45
  298.4 11.3 %fusion.2 = (bf16[512,3072]{1,0:T(8,128)(2,1)}, bf16[512,3072]{1,0:T(8,128)(2,1)}, bf16[512,3072]{1,0:T(8,128)(2,1)}) fusion(f32[512,3072]{1,0:T(8,128)} %fusion.92, f32[3072,512]{0,1:T(8,128)} %fusion.45, bf16[512,1024]{1,0:T(8,128)(2,1)S(1)} %copy-done.55, bf16[1024,3072]{1,0:T(8,128)(2,1)S(1)} %bitcast.475), kind=kOutput, calls=%fused_computation.3 | convolution fusion | flops 3246391296 | bytes 29360128 | tf_op jit(solution)/shard_map/dot_general | solution.py:19
  309.7 8.7 %reshape.518 = bf16[512,2,2,768]{3,2,1,0:T(2,128)(2,1)} reshape(bf16[512,3072]{1,0:T(8,128)(2,1)} %get-tuple-element.51) | data formatting | bytes 6291456 | tf_op jit(solution)/shard_map/reshape | solution.py:62
  318.3 8.8 %fusion.27 = bf16[1,512,1024]{2,1,0:T(8,128)(2,1)} fusion(f32[512,1024]{1,0:T(8,128)} %copy-done.41, bf16[512,3072]{1,0:T(8,128)(2,1)} %get-tuple-element.51, bf16[3072,1024]{1,0:T(8,128)(2,1)} %bitcast.477), kind=kOutput, calls=%fused_computation.111 | convolution fusion | flops 3222274048 | bytes 12582912 | tf_op jit(solution)/shard_map/dot_general | solution.py:19
  327.2 9.2 %constant_dynamic-slice_fusion.1 = (bf16[512,2,1,768]{3,2,1,0:T(2,128)(2,1)}, bf16[512,2,1,768]{3,2,1,0:T(2,128)(2,1)}) fusion(bf16[512,2,2,768]{3,2,1,0:T(2,128)(2,1)S(1)} %copy-done.19, s32[]{:T(128)S(6)} %select_n.749, s32[]{:T(128)S(6)} %select_n.750), kind=kLoop, calls=%fused_computation.259 | loop fusion | bytes 6291464 | tf_op jit(solution)/shard_map/jit(dynamic_index_in_dim)/dynamic_slice | solution.py:53
  336.4 8.2 copy.74
  344.5 7.4 fusion.93
  352.0 3.5 convolution_convert_fusion
  355.4 6.3 multiply_reduce_fusion
  369.0 4.5 collective-permute-start.43
  373.6 17.5 %shard_map.240 = (bf16[512,1024]{1,0:T(8,128)(2,1)S(1)}, f32[1,128]{1,0:T(1,128)S(1)}, bf16[512,512]{1,0:T(8,128)(2,1)S(1)}, f32[512,512]{1,0:T(8,128)S(1)}, bf1...) custom-call(bf16[512,2048]{1,0:T(8,128)(2,1)S(1)} %copy-done.2, bf16[512,1024]{1,0:T(8,128)(2,1)S(1)} %copy-done.14, ...), custom_call_target="tpu_custom_call" | custom-call | flops 10737418240 | bytes 10485760 | tf_op jit(solution)/shard_map/pallas_call | solution.py:324
  394.0 17.9 %shard_map.242 = (bf16[512,1024]{1,0:T(8,128)(2,1)S(1)}, f32[1,128]{1,0:T(1,128)S(1)}, bf16[512,512]{1,0:T(8,128)(2,1)S(1)}, f32[512,512]{1,0:T(8,128)S(1)}, bf1...) custom-call(bf16[512,2048]{1,0:T(8,128)(2,1)S(1)} %copy-done.2, bf16[512,1024]{1,0:T(8,128)(2,1)S(1)} %copy-done.14, ...), custom_call_target="tpu_custom_call" | custom-call | flops 10737418240 | bytes 10485760 | tf_op jit(solution)/shard_map/pallas_call | solution.py:324
  419.8 3.5 convolution_convert_fusion.1
  437.0 3.4 collective-permute-start.22
  443.0 4.0 collective-permute-start.23
  447.0 3.5 convolution_convert_fusion.2
  450.7 8.4 %copy.73 = bf16[512,2,1,768]{0,3,1,2:T(8,128)(2,1)} copy(bf16[512,2,1,768]{3,2,1,0:T(2,128)(2,1)} %get-tuple-element.62) | data formatting | bytes 3145728
  483.8 19.5 %collective-permute-done.44 = bf16[1,512,1024]{2,1,0:T(8,128)(2,1)S(1)} collective-permute-done((bf16[1,512,1024]{2,1,0:T(8,128)(2,1)S(1)}, bf16[1,512,1024]{2,1,0:T(8,128)(2,1)S(1)}, u32[]{:S(2)}, u32[]{:S(2)}) %collective-permute-start.44) | collective-permute-done | bytes 1048608 | tf_op jit(solution)/shard_map/ppermute | solution.py:24
  505.1 3.9 add_convert_fusion
  514.7 3.7 add_convert_fusion.2
  519.6 6.1 collective-permute-done.28
  527.7 4.4 collective-permute-done.46
  533.3 14.9 %collective-permute-done.36 = bf16[1,256,2048]{2,1,0:T(8,128)(2,1)S(1)} collective-permute-done((bf16[1,256,2048]{2,1,0:T(8,128)(2,1)S(1)}, bf16[1,256,2048]{2,1,0:T(8,128)(2,1)S(1)}, u32[]{:S(2)}, u32[]{:S(2)}) %collective-permute-start.36) | collective-permute-done | bytes 1048608 | tf_op jit(solution)/shard_map/ppermute | solution.py:24
  550.7 5.0 collective-permute-done.47
  556.4 5.2 collective-permute-done.48
  562.8 3.2 collective-permute-start.49
  566.1 6.7 collective-permute-done.37
  575.2 5.0 collective-permute-done.30
  585.4 7.8 collective-permute-done.31
  593.2 9.7 %collective-permute-done.39 = bf16[32,2048]{1,0:T(8,128)(2,1)S(1)} collective-permute-done((bf16[32,2048]{1,0:T(8,128)(2,1)S(1)}, bf16[32,2048]{1,0:T(8,128)(2,1)S(1)}, u32[]{:S(2)}, u32[]{:S(2)}) %collective-permute-start.39) | collective-permute-done | bytes 131104 | tf_op jit(solution)/shard_map/ppermute | solution.py:24
  606.7 8.9 %collective-permute-done.60 = bf16[1,256,3072]{2,1,0:T(8,128)(2,1)S(1)} collective-permute-done((bf16[1,256,3072]{2,1,0:T(8,128)(2,1)S(1)}, bf16[1,256,3072]{2,1,0:T(8,128)(2,1)S(1)}, u32[]{:S(2)}, u32[]{:S(2)}) %collective-permute-start.60) | collective-permute-done | bytes 1572896 | tf_op jit(solution)/shard_map/ppermute | solution.py:24
  617.3 31.1 %collective-permute-done.52 = bf16[1,256,3072]{2,1,0:T(8,128)(2,1)S(1)} collective-permute-done((bf16[1,256,3072]{2,1,0:T(8,128)(2,1)S(1)}, bf16[1,256,3072]{2,1,0:T(8,128)(2,1)S(1)}, u32[]{:S(2)}, u32[]{:S(2)}) %collective-permute-start.52) | collective-permute-done | bytes 1572896 | tf_op jit(solution)/shard_map/ppermute | solution.py:24
  652.9 5.2 collective-permute-done.33
  659.8 4.7 collective-permute-done.41
  671.2 25.7 %collective-permute-done.34 = bf16[128,2048]{1,0:T(8,128)(2,1)S(1)} collective-permute-done((bf16[128,2048]{1,0:T(8,128)(2,1)S(1)}, bf16[128,2048]{1,0:T(8,128)(2,1)S(1)}, u32[]{:S(2)}, u32[]{:S(2)}) %collective-permute-start.34) | collective-permute-done | bytes 524320 | tf_op jit(solution)/shard_map/ppermute | solution.py:24
  697.4 8.8 %collective-permute-done.42 = bf16[128,2048]{1,0:T(8,128)(2,1)S(1)} collective-permute-done((bf16[128,2048]{1,0:T(8,128)(2,1)S(1)}, bf16[128,2048]{1,0:T(8,128)(2,1)S(1)}, u32[]{:S(2)}, u32[]{:S(2)}) %collective-permute-start.42) | collective-permute-done | bytes 524320 | tf_op jit(solution)/shard_map/ppermute | solution.py:24
  717.1 4.1 collective-permute-done.54
  723.0 13.4 %collective-permute-done.71 = bf16[96,1024]{1,0:T(8,128)(2,1)S(1)} collective-permute-done((bf16[96,1024]{1,0:T(8,128)(2,1)S(1)}, bf16[96,1024]{1,0:T(8,128)(2,1)S(1)}, u32[]{:S(2)}, u32[]{:S(2)}) %collective-permute-start.71) | collective-permute-done | bytes 196640 | tf_op jit(solution)/shard_map/ppermute | solution.py:24
  736.6 8.3 %collective-permute-done.63 = bf16[32,3072]{1,0:T(8,128)(2,1)S(1)} collective-permute-done((bf16[32,3072]{1,0:T(8,128)(2,1)S(1)}, bf16[32,3072]{1,0:T(8,128)(2,1)S(1)}, u32[]{:S(2)}, u32[]{:S(2)}) %collective-permute-start.63) | collective-permute-done | bytes 196640 | tf_op jit(solution)/shard_map/ppermute | solution.py:24
  745.0 8.3 %collective-permute-done.55 = bf16[32,3072]{1,0:T(8,128)(2,1)S(1)} collective-permute-done((bf16[32,3072]{1,0:T(8,128)(2,1)S(1)}, bf16[32,3072]{1,0:T(8,128)(2,1)S(1)}, u32[]{:S(2)}, u32[]{:S(2)}) %collective-permute-start.55) | collective-permute-done | bytes 196640 | tf_op jit(solution)/shard_map/ppermute | solution.py:24
  753.4 4.8 collective-permute-done.72
  758.4 5.5 collective-permute-done.64
  766.2 8.3 %collective-permute-done.73 = bf16[192,1024]{1,0:T(8,128)(2,1)S(1)} collective-permute-done((bf16[192,1024]{1,0:T(8,128)(2,1)S(1)}, bf16[192,1024]{1,0:T(8,128)(2,1)S(1)}, u32[]{:S(2)}, u32[]{:S(2)}) %collective-permute-start.73) | collective-permute-done | bytes 393248 | tf_op jit(solution)/shard_map/ppermute | solution.py:24
  775.8 7.2 collective-permute-done.65
  784.2 4.9 collective-permute-done.57
  790.4 4.8 collective-permute-done.74
  797.7 14.4 %collective-permute-done.66 = bf16[128,3072]{1,0:T(8,128)(2,1)S(1)} collective-permute-done((bf16[128,3072]{1,0:T(8,128)(2,1)S(1)}, bf16[128,3072]{1,0:T(8,128)(2,1)S(1)}, u32[]{:S(2)}, u32[]{:S(2)}) %collective-permute-start.66) | collective-permute-done | bytes 786464 | tf_op jit(solution)/shard_map/ppermute | solution.py:24
  814.5 9.0 %collective-permute-done.58 = bf16[128,3072]{1,0:T(8,128)(2,1)S(1)} collective-permute-done((bf16[128,3072]{1,0:T(8,128)(2,1)S(1)}, bf16[128,3072]{1,0:T(8,128)(2,1)S(1)}, u32[]{:S(2)}, u32[]{:S(2)}) %collective-permute-start.58) | collective-permute-done | bytes 786464 | tf_op jit(solution)/shard_map/ppermute | solution.py:24
  (490 shorter events, 213.2 us)
Async XLA Ops:
  0.7 159.3 %collective-permute-start.12 = (bf16[256,3072]{1,0:T(8,128)(2,1)}, bf16[256,3072]{1,0:T(8,128)(2,1)}, u32[]{:S(2)}, u32[]{:S(2)}) collective-permute-start(bf16[256,3072]{1,0:T(8,128)(2,1)} %param.25), channel_id=1, source_target_pairs={{0,2},{1,3},{2,0},{3,1},{4,6},{5,7},{6,4},{7,5},{8,10},{9,11},{10,... | collective-permute-start | bytes 4718600 | tf_op jit(solution)/shard_map/ppermute | solution.py:24
  3.7 158.8 %collective-permute-start.14 = (bf16[256,3072]{1,0:T(8,128)(2,1)}, bf16[256,3072]{1,0:T(8,128)(2,1)}, u32[]{:S(2)}, u32[]{:S(2)}) collective-permute-start(bf16[256,3072]{1,0:T(8,128)(2,1)} %param.26), channel_id=1, source_target_pairs={{0,2},{1,3},{2,0},{3,1},{4,6},{5,7},{6,4},{7,5},{8,10},{9,11},{10,... | collective-permute-start | bytes 4718600 | tf_op jit(solution)/shard_map/ppermute | solution.py:24
  3.8 103.6 %collective-permute-start.4 = (bf16[256,1024]{1,0:T(8,128)(2,1)}, bf16[256,1024]{1,0:T(8,128)(2,1)S(1)}, u32[]{:S(2)}, u32[]{:S(2)}) collective-permute-start(bf16[256,1024]{1,0:T(8,128)(2,1)} %param.19), channel_id=1, source_target_pairs={{0,2},{1,3},{2,0},{3,1},{4,6},{5,7},{6,4},{7,5},{8,10},{9,11},{10,... | collective-permute-start | bytes 1572872 | tf_op jit(solution)/shard_map/ppermute | solution.py:24
  5.7 102.0 %collective-permute-start.7 = (bf16[256,1024]{1,0:T(8,128)(2,1)}, bf16[256,1024]{1,0:T(8,128)(2,1)}, u32[]{:S(2)}, u32[]{:S(2)}) collective-permute-start(bf16[256,1024]{1,0:T(8,128)(2,1)} %param.20), channel_id=1, source_target_pairs={{0,2},{1,3},{2,0},{3,1},{4,6},{5,7},{6,4},{7,5},{8,10},{9,11},{10,... | collective-permute-start | bytes 1572872 | tf_op jit(solution)/shard_map/ppermute | solution.py:24
  6.6 88.0 %collective-permute-start = (bf16[1,576]{1,0:T(2,128)(2,1)S(1)}, bf16[1,576]{1,0:T(2,128)(2,1)S(1)}, u32[]{:S(2)}, u32[]{:S(2)}) collective-permute-start(bf16[1,576]{1,0:T(2,128)(2,1)S(1)} %broadcast_in_dim.14), channel_id=1, source_target_pairs={{0,2},{1,3},{2,0},{3,1},{4,6},{5,7},{6,4},{7,5},{8,10},{9,11},{10,... | collective-permute-start | bytes 3464 | tf_op jit(solution)/shard_map/ppermute | solution.py:24
  94.6 7.6 collective-permute-start.1
  102.2 26.1 %collective-permute-start.2 = (bf16[256,2048]{1,0:T(8,128)(2,1)S(1)}, bf16[256,2048]{1,0:T(8,128)(2,1)}, u32[]{:S(2)}, u32[]{:S(2)}) collective-permute-start(bf16[256,2048]{1,0:T(8,128)(2,1)S(1)} %copy-done.62), channel_id=1, source_target_pairs={{0,2},{1,3},{2,0},{3,1},{4,6},{5,7},{6,4},{7,5},{8,10},{9,11},{10,... | collective-permute-start | bytes 3145736 | tf_op jit(solution)/shard_map/ppermute | solution.py:24
  107.4 43.2 %collective-permute-start.10 = (bf16[512,1024]{1,0:T(8,128)(2,1)S(1)}, bf16[512,1024]{1,0:T(8,128)(2,1)S(1)}, u32[]{:S(2)}, u32[]{:S(2)}) collective-permute-start(bf16[512,1024]{1,0:T(8,128)(2,1)S(1)} %copy-done.63), channel_id=1, source_target_pairs={{0,2},{1,3},{2,0},{3,1},{4,6},{5,7},{6,4},{7,5},{8,10},{9,11},{10,... | collective-permute-start | bytes 3145736 | tf_op jit(solution)/shard_map/ppermute | solution.py:24
  107.7 76.3 %collective-permute-start.16 = (bf16[768,1024]{1,0:T(8,128)(2,1)}, bf16[768,1024]{1,0:T(8,128)(2,1)}, u32[]{:S(2)}, u32[]{:S(2)}) collective-permute-start(bf16[768,1024]{1,0:T(8,128)(2,1)} %param.27), channel_id=1, source_target_pairs={{0,2},{1,3},{2,0},{3,1},{4,6},{5,7},{6,4},{7,5},{8,10},{9,11},{10,... | collective-permute-start | bytes 4718600 | tf_op jit(solution)/shard_map/ppermute | solution.py:24
  128.3 24.7 %collective-permute-start.8 = (bf16[2,256,1024]{2,1,0:T(8,128)(2,1)S(1)}, bf16[2,256,1024]{2,1,0:T(8,128)(2,1)S(1)}, u32[]{:S(2)}, u32[]{:S(2)}) collective-permute-start(bf16[2,256,1024]{2,1,0:T(8,128)(2,1)S(1)} %pad_maximum_fusion.19), channel_id=1, source_target_pairs={{0,1},{1,0},{2,3},{3,2},{4,5},{5,4},{6,7},{7,6},{8,9},{9,8},{10,11... | collective-permute-start | bytes 3145736 | tf_op jit(solution)/shard_map/ppermute | solution.py:24
  153.0 73.0 %collective-permute-start.11 = (bf16[2,512,1024]{2,1,0:T(8,128)(2,1)}, bf16[2,512,1024]{2,1,0:T(8,128)(2,1)}, u32[]{:S(2)}, u32[]{:S(2)}) collective-permute-start(bf16[2,512,1024]{2,1,0:T(8,128)(2,1)} %pad_maximum_fusion.11), channel_id=1, source_target_pairs={{0,1},{1,0},{2,3},{3,2},{4,5},{5,4},{6,7},{7,6},{8,9},{9,8},{10,11... | collective-permute-start | bytes 6291464 | tf_op jit(solution)/shard_map/ppermute | solution.py:24
  154.1 36.6 %collective-permute-start.3 = (bf16[2,256,2048]{2,1,0:T(8,128)(2,1)S(1)}, bf16[2,256,2048]{2,1,0:T(8,128)(2,1)S(1)}, u32[]{:S(2)}, u32[]{:S(2)}) collective-permute-start(bf16[2,256,2048]{2,1,0:T(8,128)(2,1)S(1)} %pad_maximum_fusion.8), channel_id=1, source_target_pairs={{0,1},{1,0},{2,3},{3,2},{4,5},{5,4},{6,7},{7,6},{8,9},{9,8},{10,11... | collective-permute-start | bytes 6291464 | tf_op jit(solution)/shard_map/ppermute | solution.py:24
  159.9 41.2 %collective-permute-start.9 = (bf16[512,1024]{1,0:T(8,128)(2,1)S(1)}, bf16[512,1024]{1,0:T(8,128)(2,1)S(1)}, u32[]{:S(2)}, u32[]{:S(2)}) collective-permute-start(bf16[512,1024]{1,0:T(8,128)(2,1)S(1)} %convolution_convert_fusion.7.v), channel_id=1, source_target_pairs={{0,1},{1,2},{2,3},{4,5},{5,6},{6,7},{8,9},{9,10},{10,11},{12,13},{... | collective-permute-start | bytes 3145736 | tf_op jit(solution)/shard_map/ppermute | solution.py:102
  162.5 38.7 %collective-permute-start.6 = (bf16[512,1024]{1,0:T(8,128)(2,1)S(1)}, bf16[512,1024]{1,0:T(8,128)(2,1)S(1)}, u32[]{:S(2)}, u32[]{:S(2)}) collective-permute-start(bf16[512,1024]{1,0:T(8,128)(2,1)S(1)} %shard_map.238.k), channel_id=1, source_target_pairs={{0,1},{1,2},{2,3},{4,5},{5,6},{6,7},{8,9},{9,10},{10,11},{12,13},{... | collective-permute-start | bytes 3145736 | tf_op jit(solution)/shard_map/ppermute | solution.py:102
  184.0 90.6 %collective-permute-start.13 = (bf16[2,256,3072]{2,1,0:T(8,128)(2,1)}, bf16[2,256,3072]{2,1,0:T(8,128)(2,1)}, u32[]{:S(2)}, u32[]{:S(2)}) collective-permute-start(bf16[2,256,3072]{2,1,0:T(8,128)(2,1)} %pad_maximum_fusion.5), channel_id=1, source_target_pairs={{0,1},{1,0},{2,3},{3,2},{4,5},{5,4},{6,7},{7,6},{8,9},{9,8},{10,11... | collective-permute-start | bytes 9437192 | tf_op jit(solution)/shard_map/ppermute | solution.py:24
  190.7 79.8 %collective-permute-start.15 = (bf16[2,256,3072]{2,1,0:T(8,128)(2,1)}, bf16[2,256,3072]{2,1,0:T(8,128)(2,1)}, u32[]{:S(2)}, u32[]{:S(2)}) collective-permute-start(bf16[2,256,3072]{2,1,0:T(8,128)(2,1)} %pad_maximum_fusion.6), channel_id=1, source_target_pairs={{0,1},{1,0},{2,3},{3,2},{4,5},{5,4},{6,7},{7,6},{8,9},{9,8},{10,11... | collective-permute-start | bytes 9437192 | tf_op jit(solution)/shard_map/ppermute | solution.py:24
  201.1 86.9 %collective-permute-start.17 = (bf16[2,768,1024]{2,1,0:T(8,128)(2,1)}, bf16[2,768,1024]{2,1,0:T(8,128)(2,1)}, u32[]{:S(2)}, u32[]{:S(2)}) collective-permute-start(bf16[2,768,1024]{2,1,0:T(8,128)(2,1)} %pad_maximum_fusion.7), channel_id=1, source_target_pairs={{0,1},{1,0},{2,3},{3,2},{4,5},{5,4},{6,7},{7,6},{8,9},{9,8},{10,11... | collective-permute-start | bytes 9437192 | tf_op jit(solution)/shard_map/ppermute | solution.py:24
  369.0 104.6 %collective-permute-start.43 = (bf16[1024,1024]{1,0:T(8,128)(2,1)}, bf16[1024,1024]{1,0:T(8,128)(2,1)}, u32[]{:S(2)}, u32[]{:S(2)}) collective-permute-start(bf16[1024,1024]{1,0:T(8,128)(2,1)} %convolution_convert_fusion.6), channel_id=1, source_target_pairs={{0,1},{1,0},{2,3},{3,2},{4,5},{5,4},{6,7},{7,6},{8,9},{9,8},{10,11... | collective-permute-start | bytes 6291464 | tf_op jit(solution)/shard_map/ppermute | solution.py:24
  391.1 32.1 %collective-permute-start.18 = (bf16[512,512]{1,0:T(8,128)(2,1)S(1)}, bf16[512,512]{1,0:T(8,128)(2,1)S(1)}, u32[]{:S(2)}, u32[]{:S(2)}) collective-permute-start(bf16[512,512]{1,0:T(8,128)(2,1)S(1)} %get-tuple-element.31), channel_id=1, source_target_pairs={{1,0},{2,1},{3,2},{5,4},{6,5},{7,6},{9,8},{10,9},{11,10},{13,12},{... | collective-permute-start | bytes 1572872 | tf_op jit(solution)/shard_map/ppermute | solution.py:102
  392.4 34.0 %collective-permute-start.19 = (bf16[512,512]{1,0:T(8,128)(2,1)S(1)}, bf16[512,512]{1,0:T(8,128)(2,1)}, u32[]{:S(2)}, u32[]{:S(2)}) collective-permute-start(bf16[512,512]{1,0:T(8,128)(2,1)S(1)} %get-tuple-element.34), channel_id=1, source_target_pairs={{1,0},{2,1},{3,2},{5,4},{6,5},{7,6},{9,8},{10,9},{11,10},{13,12},{... | collective-permute-start | bytes 1572872 | tf_op jit(solution)/shard_map/ppermute | solution.py:102
  412.0 16.4 %collective-permute-start.20 = (bf16[512,512]{1,0:T(8,128)(2,1)S(1)}, bf16[512,512]{1,0:T(8,128)(2,1)}, u32[]{:S(2)}, u32[]{:S(2)}) collective-permute-start(bf16[512,512]{1,0:T(8,128)(2,1)S(1)} %get-tuple-element.37), channel_id=1, source_target_pairs={{1,0},{2,1},{3,2},{5,4},{6,5},{7,6},{9,8},{10,9},{11,10},{13,12},{... | collective-permute-start | bytes 1572872 | tf_op jit(solution)/shard_map/ppermute | solution.py:102
  413.3 18.9 %collective-permute-start.21 = (bf16[512,512]{1,0:T(8,128)(2,1)S(1)}, bf16[512,512]{1,0:T(8,128)(2,1)}, u32[]{:S(2)}, u32[]{:S(2)}) collective-permute-start(bf16[512,512]{1,0:T(8,128)(2,1)S(1)} %get-tuple-element.40), channel_id=1, source_target_pairs={{1,0},{2,1},{3,2},{5,4},{6,5},{7,6},{9,8},{10,9},{11,10},{13,12},{... | collective-permute-start | bytes 1572872 | tf_op jit(solution)/shard_map/ppermute | solution.py:102
  443.0 34.2 %collective-permute-start.27 = (bf16[512,2048]{1,0:T(8,128)(2,1)}, bf16[512,2048]{1,0:T(8,128)(2,1)}, u32[]{:S(2)}, u32[]{:S(2)}) collective-permute-start(bf16[512,2048]{1,0:T(8,128)(2,1)} %convolution_convert_fusion.5), channel_id=1, source_target_pairs={{0,1},{1,0},{2,3},{3,2},{4,5},{5,4},{6,7},{7,6},{8,9},{9,8},{10,11... | collective-permute-start | bytes 6291464 | tf_op jit(solution)/shard_map/ppermute | solution.py:24
  443.0 16.1 %collective-permute-start.23 = (f32[2304]{0:T(1024)S(1)}, f32[2304]{0:T(1024)S(1)}, u32[]{:S(2)}, u32[]{:S(2)}) collective-permute-start(f32[2304]{0:T(1024)S(1)} %fusion.81), channel_id=1, source_target_pairs={{0,2},{1,3},{2,0},{3,1},{4,6},{5,7},{6,4},{7,5},{8,10},{9,11},{10,... | collective-permute-start | bytes 27656 | tf_op jit(solution)/shard_map/ppermute | solution.py:24
  450.5 53.2 %collective-permute-start.67 = (bf16[1536,1024]{1,0:T(8,128)(2,1)}, bf16[1536,1024]{1,0:T(8,128)(2,1)}, u32[]{:S(2)}, u32[]{:S(2)}) collective-permute-start(bf16[1536,1024]{1,0:T(8,128)(2,1)} %convolution_convert_fusion.2), channel_id=1, source_target_pairs={{0,1},{1,0},{2,3},{3,2},{4,5},{5,4},{6,7},{7,6},{8,9},{9,8},{10,11... | collective-permute-start | bytes 9437192 | tf_op jit(solution)/shard_map/ppermute | solution.py:24
  463.1 18.3 %collective-permute-start.35 = (bf16[512,2048]{1,0:T(8,128)(2,1)S(1)}, bf16[512,2048]{1,0:T(8,128)(2,1)S(1)}, u32[]{:S(2)}, u32[]{:S(2)}) collective-permute-start(bf16[512,2048]{1,0:T(8,128)(2,1)S(1)} %convolution_convert_fusion.4), channel_id=1, source_target_pairs={{0,1},{1,0},{2,3},{3,2},{4,5},{5,4},{6,7},{7,6},{8,9},{9,8},{10,11... | collective-permute-start | bytes 6291464 | tf_op jit(solution)/shard_map/ppermute | solution.py:24
  472.4 36.8 %collective-permute-start.59 = (bf16[512,3072]{1,0:T(8,128)(2,1)S(1)}, bf16[512,3072]{1,0:T(8,128)(2,1)S(1)}, u32[]{:S(2)}, u32[]{:S(2)}) collective-permute-start(bf16[512,3072]{1,0:T(8,128)(2,1)S(1)} %copy-done.80), channel_id=1, source_target_pairs={{0,1},{1,0},{2,3},{3,2},{4,5},{5,4},{6,7},{7,6},{8,9},{9,8},{10,11... | collective-permute-start | bytes 9437192 | tf_op jit(solution)/shard_map/ppermute | solution.py:24
  473.6 39.3 %collective-permute-start.51 = (bf16[512,3072]{1,0:T(8,128)(2,1)S(1)}, bf16[512,3072]{1,0:T(8,128)(2,1)}, u32[]{:S(2)}, u32[]{:S(2)}) collective-permute-start(bf16[512,3072]{1,0:T(8,128)(2,1)S(1)} %copy-done.81), channel_id=1, source_target_pairs={{0,1},{1,0},{2,3},{3,2},{4,5},{5,4},{6,7},{7,6},{8,9},{9,8},{10,11... | collective-permute-start | bytes 9437192 | tf_op jit(solution)/shard_map/ppermute | solution.py:24
  477.1 26.1 %collective-permute-start.44 = (bf16[1,512,1024]{2,1,0:T(8,128)(2,1)S(1)}, bf16[1,512,1024]{2,1,0:T(8,128)(2,1)S(1)}, u32[]{:S(2)}, u32[]{:S(2)}) collective-permute-start(bf16[1,512,1024]{2,1,0:T(8,128)(2,1)S(1)} %dynamic-slice_bitcast_fusion.3), channel_id=1, source_target_pairs={{0,2},{1,3},{2,0},{3,1},{4,6},{5,7},{6,4},{7,5},{8,10},{9,11},{10,... | collective-permute-start | bytes 3145736 | tf_op jit(solution)/shard_map/ppermute | solution.py:24
  481.4 44.3 %collective-permute-start.28 = (bf16[1,256,2048]{2,1,0:T(8,128)(2,1)S(1)}, bf16[1,256,2048]{2,1,0:T(8,128)(2,1)S(1)}, u32[]{:S(2)}, u32[]{:S(2)}) collective-permute-start(bf16[1,256,2048]{2,1,0:T(8,128)(2,1)S(1)} %dynamic-slice_bitcast_fusion.5), channel_id=1, source_target_pairs={{0,2},{1,3},{2,0},{3,1},{4,6},{5,7},{6,4},{7,5},{8,10},{9,11},{10,... | collective-permute-start | bytes 3145736 | tf_op jit(solution)/shard_map/ppermute | solution.py:24
  503.2 44.9 %collective-permute-start.36 = (bf16[1,256,2048]{2,1,0:T(8,128)(2,1)S(1)}, bf16[1,256,2048]{2,1,0:T(8,128)(2,1)S(1)}, u32[]{:S(2)}, u32[]{:S(2)}) collective-permute-start(bf16[1,256,2048]{2,1,0:T(8,128)(2,1)S(1)} %dynamic-slice_bitcast_fusion.4), channel_id=1, source_target_pairs={{0,2},{1,3},{2,0},{3,1},{4,6},{5,7},{6,4},{7,5},{8,10},{9,11},{10,... | collective-permute-start | bytes 3145736 | tf_op jit(solution)/shard_map/ppermute | solution.py:24
  503.8 14.7 %collective-permute-start.45 = (bf16[256,1024]{1,0:T(8,128)(2,1)S(1)}, bf16[256,1024]{1,0:T(8,128)(2,1)S(1)}, u32[]{:S(2)}, u32[]{:S(2)}) collective-permute-start(bf16[256,1024]{1,0:T(8,128)(2,1)S(1)} %dynamic-slice_bitcast_fusion.9), channel_id=1, source_target_pairs={{0,4},{4,0},{8,12},{12,8},{16,20},{20,16},{24,28},{28,24},{1,5},{5... | collective-permute-start | bytes 1572872 | tf_op jit(solution)/shard_map/ppermute | solution.py:24
  509.2 93.8 %collective-permute-start.68 = (bf16[1,768,1024]{2,1,0:T(8,128)(2,1)S(1)}, bf16[1,768,1024]{2,1,0:T(8,128)(2,1)S(1)}, u32[]{:S(2)}, u32[]{:S(2)}) collective-permute-start(bf16[1,768,1024]{2,1,0:T(8,128)(2,1)S(1)} %dynamic-slice_bitcast_fusion), channel_id=1, source_target_pairs={{0,2},{1,3},{2,0},{3,1},{4,6},{5,7},{6,4},{7,5},{8,10},{9,11},{10,... | collective-permute-start | bytes 4718600 | tf_op jit(solution)/shard_map/ppermute | solution.py:24
  512.9 102.7 %collective-permute-start.60 = (bf16[1,256,3072]{2,1,0:T(8,128)(2,1)S(1)}, bf16[1,256,3072]{2,1,0:T(8,128)(2,1)S(1)}, u32[]{:S(2)}, u32[]{:S(2)}) collective-permute-start(bf16[1,256,3072]{2,1,0:T(8,128)(2,1)S(1)} %dynamic-slice_bitcast_fusion.1), channel_id=1, source_target_pairs={{0,2},{1,3},{2,0},{3,1},{4,6},{5,7},{6,4},{7,5},{8,10},{9,11},{10,... | collective-permute-start | bytes 4718600 | tf_op jit(solution)/shard_map/ppermute | solution.py:24
  518.5 129.8 %collective-permute-start.52 = (bf16[1,256,3072]{2,1,0:T(8,128)(2,1)S(1)}, bf16[1,256,3072]{2,1,0:T(8,128)(2,1)S(1)}, u32[]{:S(2)}, u32[]{:S(2)}) collective-permute-start(bf16[1,256,3072]{2,1,0:T(8,128)(2,1)S(1)} %dynamic-slice_bitcast_fusion.2), channel_id=1, source_target_pairs={{0,2},{1,3},{2,0},{3,1},{4,6},{5,7},{6,4},{7,5},{8,10},{9,11},{10,... | collective-permute-start | bytes 4718600 | tf_op jit(solution)/shard_map/ppermute | solution.py:24
  532.1 30.7 %collective-permute-start.29 = (bf16[128,2048]{1,0:T(8,128)(2,1)S(1)}, bf16[128,2048]{1,0:T(8,128)(2,1)S(1)}, u32[]{:S(2)}, u32[]{:S(2)}) collective-permute-start(bf16[128,2048]{1,0:T(8,128)(2,1)S(1)} %dynamic-slice_bitcast_fusion.11), channel_id=1, source_target_pairs={{0,4},{4,0},{8,12},{12,8},{16,20},{20,16},{24,28},{28,24},{1,5},{5... | collective-permute-start | bytes 1572872 | tf_op jit(solution)/shard_map/ppermute | solution.py:24
  561.7 11.1 %collective-permute-start.37 = (bf16[128,2048]{1,0:T(8,128)(2,1)S(1)}, bf16[128,2048]{1,0:T(8,128)(2,1)S(1)}, u32[]{:S(2)}, u32[]{:S(2)}) collective-permute-start(bf16[128,2048]{1,0:T(8,128)(2,1)S(1)} %dynamic-slice_bitcast_fusion.10), channel_id=1, source_target_pairs={{0,4},{4,0},{8,12},{12,8},{16,20},{20,16},{24,28},{28,24},{1,5},{5... | collective-permute-start | bytes 1572872 | tf_op jit(solution)/shard_map/ppermute | solution.py:24
  562.8 11.3 %collective-permute-start.49 = (bf16[128,1024]{1,0:T(8,128)(2,1)S(1)}, bf16[128,1024]{1,0:T(8,128)(2,1)S(1)}, u32[]{:S(2)}, u32[]{:S(2)}) collective-permute-start(bf16[128,1024]{1,0:T(8,128)(2,1)S(1)} %bitcast.532), channel_id=1, source_target_pairs={{0,8},{4,12},{8,0},{12,4},{16,24},{20,28},{24,16},{28,20},{1,9},{5... | collective-permute-start | bytes 786440 | tf_op jit(solution)/shard_map/ppermute | solution.py:24
  574.1 9.9 %collective-permute-start.38 = (bf16[64,2048]{1,0:T(8,128)(2,1)S(1)}, bf16[64,2048]{1,0:T(8,128)(2,1)S(1)}, u32[]{:S(2)}, u32[]{:S(2)}) collective-permute-start(bf16[64,2048]{1,0:T(8,128)(2,1)S(1)} %dynamic-slice_bitcast_fusion.16), channel_id=1, source_target_pairs={{0,8},{4,12},{8,0},{12,4},{16,24},{20,28},{24,16},{28,20},{1,9},{5... | collective-permute-start | bytes 786440 | tf_op jit(solution)/shard_map/ppermute | solution.py:24
  580.1 85.4 %collective-permute-start.50 = (bf16[256,1024]{1,0:T(8,128)(2,1)S(1)}, bf16[256,1024]{1,0:T(8,128)(2,1)S(1)}, u32[]{:S(2)}, u32[]{:S(2)}) collective-permute-start(bf16[256,1024]{1,0:T(8,128)(2,1)S(1)} %bitcast.504), channel_id=1, source_target_pairs={{0,4},{4,0},{8,12},{12,8},{16,20},{20,16},{24,28},{28,24},{1,5},{5... | collective-permute-start | bytes 1572872 | tf_op jit(solution)/shard_map/ppermute | solution.py:24
  584.0 9.1 %collective-permute-start.31 = (bf16[32,2048]{1,0:T(8,128)(2,1)S(1)}, bf16[32,2048]{1,0:T(8,128)(2,1)S(1)}, u32[]{:S(2)}, u32[]{:S(2)}) collective-permute-start(bf16[32,2048]{1,0:T(8,128)(2,1)S(1)} %dynamic-slice_bitcast_fusion.23), channel_id=1, source_target_pairs={{0,16},{4,20},{8,24},{12,28},{16,0},{20,4},{24,8},{28,12},{1,17},{... | collective-permute-start | bytes 393224 | tf_op jit(solution)/shard_map/ppermute | solution.py:24
  593.2 9.7 %collective-permute-start.39 = (bf16[32,2048]{1,0:T(8,128)(2,1)S(1)}, bf16[32,2048]{1,0:T(8,128)(2,1)S(1)}, u32[]{:S(2)}, u32[]{:S(2)}) collective-permute-start(bf16[32,2048]{1,0:T(8,128)(2,1)S(1)} %dynamic-slice_bitcast_fusion.22), channel_id=1, source_target_pairs={{0,16},{4,20},{8,24},{12,28},{16,0},{20,4},{24,8},{28,12},{1,17},{... | collective-permute-start | bytes 393224 | tf_op jit(solution)/shard_map/ppermute | solution.py:24
  602.9 47.1 %collective-permute-start.32 = (bf16[32,2048]{1,0:T(8,128)(2,1)S(1)}, bf16[32,2048]{1,0:T(8,128)(2,1)S(1)}, u32[]{:S(2)}, u32[]{:S(2)}) collective-permute-start(bf16[32,2048]{1,0:T(8,128)(2,1)S(1)} %fusion.62), channel_id=1, source_target_pairs={{0,16},{4,20},{8,24},{12,28},{16,0},{20,4},{24,8},{28,12},{1,17},{... | collective-permute-start | bytes 393224 | tf_op jit(solution)/shard_map/ppermute | solution.py:24
  603.0 48.2 %collective-permute-start.40 = (bf16[32,2048]{1,0:T(8,128)(2,1)S(1)}, bf16[32,2048]{1,0:T(8,128)(2,1)S(1)}, u32[]{:S(2)}, u32[]{:S(2)}) collective-permute-start(bf16[32,2048]{1,0:T(8,128)(2,1)S(1)} %fusion.61), channel_id=1, source_target_pairs={{0,16},{4,20},{8,24},{12,28},{16,0},{20,4},{24,8},{28,12},{1,17},{... | collective-permute-start | bytes 393224 | tf_op jit(solution)/shard_map/ppermute | solution.py:24
  615.6 52.9 %collective-permute-start.69 = (bf16[384,1024]{1,0:T(8,128)(2,1)S(1)}, bf16[384,1024]{1,0:T(8,128)(2,1)S(1)}, u32[]{:S(2)}, u32[]{:S(2)}) collective-permute-start(bf16[384,1024]{1,0:T(8,128)(2,1)S(1)} %dynamic-slice_bitcast_fusion.6), channel_id=1, source_target_pairs={{0,4},{4,0},{8,12},{12,8},{16,20},{20,16},{24,28},{28,24},{1,5},{5... | collective-permute-start | bytes 2359304 | tf_op jit(solution)/shard_map/ppermute | solution.py:24
  648.3 22.2 %collective-permute-start.61 = (bf16[128,3072]{1,0:T(8,128)(2,1)S(1)}, bf16[128,3072]{1,0:T(8,128)(2,1)S(1)}, u32[]{:S(2)}, u32[]{:S(2)}) collective-permute-start(bf16[128,3072]{1,0:T(8,128)(2,1)S(1)} %dynamic-slice_bitcast_fusion.7), channel_id=1, source_target_pairs={{0,4},{4,0},{8,12},{12,8},{16,20},{20,16},{24,28},{28,24},{1,5},{5... | collective-permute-start | bytes 2359304 | tf_op jit(solution)/shard_map/ppermute | solution.py:24
  650.0 58.2 %collective-permute-start.53 = (bf16[128,3072]{1,0:T(8,128)(2,1)S(1)}, bf16[128,3072]{1,0:T(8,128)(2,1)S(1)}, u32[]{:S(2)}, u32[]{:S(2)}) collective-permute-start(bf16[128,3072]{1,0:T(8,128)(2,1)S(1)} %dynamic-slice_bitcast_fusion.8), channel_id=1, source_target_pairs={{0,4},{4,0},{8,12},{12,8},{16,20},{20,16},{24,28},{28,24},{1,5},{5... | collective-permute-start | bytes 2359304 | tf_op jit(solution)/shard_map/ppermute | solution.py:24
  664.4 32.5 %collective-permute-start.34 = (bf16[128,2048]{1,0:T(8,128)(2,1)S(1)}, bf16[128,2048]{1,0:T(8,128)(2,1)S(1)}, u32[]{:S(2)}, u32[]{:S(2)}) collective-permute-start(bf16[128,2048]{1,0:T(8,128)(2,1)S(1)} %bitcast.505), channel_id=1, source_target_pairs={{0,4},{4,0},{8,12},{12,8},{16,20},{20,16},{24,28},{28,24},{1,5},{5... | collective-permute-start | bytes 1572872 | tf_op jit(solution)/shard_map/ppermute | solution.py:24
  665.6 40.7 %collective-permute-start.42 = (bf16[128,2048]{1,0:T(8,128)(2,1)S(1)}, bf16[128,2048]{1,0:T(8,128)(2,1)S(1)}, u32[]{:S(2)}, u32[]{:S(2)}) collective-permute-start(bf16[128,2048]{1,0:T(8,128)(2,1)S(1)} %bitcast.506), channel_id=1, source_target_pairs={{0,4},{4,0},{8,12},{12,8},{16,20},{20,16},{24,28},{28,24},{1,5},{5... | collective-permute-start | bytes 1572872 | tf_op jit(solution)/shard_map/ppermute | solution.py:24
  668.8 44.8 %collective-permute-start.70 = (bf16[192,1024]{1,0:T(8,128)(2,1)S(1)}, bf16[192,1024]{1,0:T(8,128)(2,1)S(1)}, u32[]{:S(2)}, u32[]{:S(2)}) collective-permute-start(bf16[192,1024]{1,0:T(8,128)(2,1)S(1)} %dynamic-slice_bitcast_fusion.12), channel_id=1, source_target_pairs={{0,8},{4,12},{8,0},{12,4},{16,24},{20,28},{24,16},{28,20},{1,9},{5... | collective-permute-start | bytes 1179656 | tf_op jit(solution)/shard_map/ppermute | solution.py:24
  670.7 45.2 %collective-permute-start.62 = (bf16[64,3072]{1,0:T(8,128)(2,1)S(1)}, bf16[64,3072]{1,0:T(8,128)(2,1)S(1)}, u32[]{:S(2)}, u32[]{:S(2)}) collective-permute-start(bf16[64,3072]{1,0:T(8,128)(2,1)S(1)} %dynamic-slice_bitcast_fusion.13), channel_id=1, source_target_pairs={{0,8},{4,12},{8,0},{12,4},{16,24},{20,28},{24,16},{28,20},{1,9},{5... | collective-permute-start | bytes 1179656 | tf_op jit(solution)/shard_map/ppermute | solution.py:24
  708.5 12.7 %collective-permute-start.54 = (bf16[64,3072]{1,0:T(8,128)(2,1)S(1)}, bf16[64,3072]{1,0:T(8,128)(2,1)S(1)}, u32[]{:S(2)}, u32[]{:S(2)}) collective-permute-start(bf16[64,3072]{1,0:T(8,128)(2,1)S(1)} %dynamic-slice_bitcast_fusion.14), channel_id=1, source_target_pairs={{0,8},{4,12},{8,0},{12,4},{16,24},{20,28},{24,16},{28,20},{1,9},{5... | collective-permute-start | bytes 1179656 | tf_op jit(solution)/shard_map/ppermute | solution.py:24
  713.9 22.6 %collective-permute-start.71 = (bf16[96,1024]{1,0:T(8,128)(2,1)S(1)}, bf16[96,1024]{1,0:T(8,128)(2,1)S(1)}, u32[]{:S(2)}, u32[]{:S(2)}) collective-permute-start(bf16[96,1024]{1,0:T(8,128)(2,1)S(1)} %dynamic-slice_bitcast_fusion.18), channel_id=1, source_target_pairs={{0,16},{4,20},{8,24},{12,28},{16,0},{20,4},{24,8},{28,12},{1,17},{... | collective-permute-start | bytes 589832 | tf_op jit(solution)/shard_map/ppermute | solution.py:24
  716.0 28.8 %collective-permute-start.63 = (bf16[32,3072]{1,0:T(8,128)(2,1)S(1)}, bf16[32,3072]{1,0:T(8,128)(2,1)S(1)}, u32[]{:S(2)}, u32[]{:S(2)}) collective-permute-start(bf16[32,3072]{1,0:T(8,128)(2,1)S(1)} %dynamic-slice_bitcast_fusion.19), channel_id=1, source_target_pairs={{0,16},{4,20},{8,24},{12,28},{16,0},{20,4},{24,8},{28,12},{1,17},{... | collective-permute-start | bytes 589832 | tf_op jit(solution)/shard_map/ppermute | solution.py:24
  721.3 32.0 %collective-permute-start.55 = (bf16[32,3072]{1,0:T(8,128)(2,1)S(1)}, bf16[32,3072]{1,0:T(8,128)(2,1)S(1)}, u32[]{:S(2)}, u32[]{:S(2)}) collective-permute-start(bf16[32,3072]{1,0:T(8,128)(2,1)S(1)} %dynamic-slice_bitcast_fusion.20), channel_id=1, source_target_pairs={{0,16},{4,20},{8,24},{12,28},{16,0},{20,4},{24,8},{28,12},{1,17},{... | collective-permute-start | bytes 589832 | tf_op jit(solution)/shard_map/ppermute | solution.py:24
  736.5 21.7 %collective-permute-start.72 = (bf16[96,1024]{1,0:T(8,128)(2,1)S(1)}, bf16[96,1024]{1,0:T(8,128)(2,1)S(1)}, u32[]{:S(2)}, u32[]{:S(2)}) collective-permute-start(bf16[96,1024]{1,0:T(8,128)(2,1)S(1)} %fusion.57), channel_id=1, source_target_pairs={{0,16},{4,20},{8,24},{12,28},{16,0},{20,4},{24,8},{28,12},{1,17},{... | collective-permute-start | bytes 589832 | tf_op jit(solution)/shard_map/ppermute | solution.py:24
  744.9 19.0 %collective-permute-start.64 = (bf16[32,3072]{1,0:T(8,128)(2,1)S(1)}, bf16[32,3072]{1,0:T(8,128)(2,1)S(1)}, u32[]{:S(2)}, u32[]{:S(2)}) collective-permute-start(bf16[32,3072]{1,0:T(8,128)(2,1)S(1)} %fusion.58), channel_id=1, source_target_pairs={{0,16},{4,20},{8,24},{12,28},{16,0},{20,4},{24,8},{28,12},{1,17},{... | collective-permute-start | bytes 589832 | tf_op jit(solution)/shard_map/ppermute | solution.py:24
  753.3 12.7 %collective-permute-start.56 = (bf16[32,3072]{1,0:T(8,128)(2,1)S(1)}, bf16[32,3072]{1,0:T(8,128)(2,1)S(1)}, u32[]{:S(2)}, u32[]{:S(2)}) collective-permute-start(bf16[32,3072]{1,0:T(8,128)(2,1)S(1)} %fusion.59), channel_id=1, source_target_pairs={{0,16},{4,20},{8,24},{12,28},{16,0},{20,4},{24,8},{28,12},{1,17},{... | collective-permute-start | bytes 589832 | tf_op jit(solution)/shard_map/ppermute | solution.py:24
  758.3 16.2 %collective-permute-start.73 = (bf16[192,1024]{1,0:T(8,128)(2,1)S(1)}, bf16[192,1024]{1,0:T(8,128)(2,1)S(1)}, u32[]{:S(2)}, u32[]{:S(2)}) collective-permute-start(bf16[192,1024]{1,0:T(8,128)(2,1)S(1)} %bitcast.519), channel_id=1, source_target_pairs={{0,8},{4,12},{8,0},{12,4},{16,24},{20,28},{24,16},{28,20},{1,9},{5... | collective-permute-start | bytes 1179656 | tf_op jit(solution)/shard_map/ppermute | solution.py:24
  763.9 19.0 %collective-permute-start.65 = (bf16[64,3072]{1,0:T(8,128)(2,1)S(1)}, bf16[64,3072]{1,0:T(8,128)(2,1)S(1)}, u32[]{:S(2)}, u32[]{:S(2)}) collective-permute-start(bf16[64,3072]{1,0:T(8,128)(2,1)S(1)} %bitcast.520), channel_id=1, source_target_pairs={{0,8},{4,12},{8,0},{12,4},{16,24},{20,28},{24,16},{28,20},{1,9},{5... | collective-permute-start | bytes 1179656 | tf_op jit(solution)/shard_map/ppermute | solution.py:24
  766.1 23.0 %collective-permute-start.57 = (bf16[64,3072]{1,0:T(8,128)(2,1)S(1)}, bf16[64,3072]{1,0:T(8,128)(2,1)S(1)}, u32[]{:S(2)}, u32[]{:S(2)}) collective-permute-start(bf16[64,3072]{1,0:T(8,128)(2,1)S(1)} %bitcast.521), channel_id=1, source_target_pairs={{0,8},{4,12},{8,0},{12,4},{16,24},{20,28},{24,16},{28,20},{1,9},{5... | collective-permute-start | bytes 1179656 | tf_op jit(solution)/shard_map/ppermute | solution.py:24
  774.7 20.5 %collective-permute-start.74 = (bf16[384,1024]{1,0:T(8,128)(2,1)S(1)}, bf16[384,1024]{1,0:T(8,128)(2,1)S(1)}, u32[]{:S(2)}, u32[]{:S(2)}) collective-permute-start(bf16[384,1024]{1,0:T(8,128)(2,1)S(1)} %bitcast.501), channel_id=1, source_target_pairs={{0,4},{4,0},{8,12},{12,8},{16,20},{20,16},{24,28},{28,24},{1,5},{5... | collective-permute-start | bytes 2359304 | tf_op jit(solution)/shard_map/ppermute | solution.py:24
  783.1 29.0 %collective-permute-start.66 = (bf16[128,3072]{1,0:T(8,128)(2,1)S(1)}, bf16[128,3072]{1,0:T(8,128)(2,1)S(1)}, u32[]{:S(2)}, u32[]{:S(2)}) collective-permute-start(bf16[128,3072]{1,0:T(8,128)(2,1)S(1)} %bitcast.502), channel_id=1, source_target_pairs={{0,4},{4,0},{8,12},{12,8},{16,20},{20,16},{24,28},{28,24},{1,5},{5... | collective-permute-start | bytes 2359304 | tf_op jit(solution)/shard_map/ppermute | solution.py:24
  789.3 34.3 %collective-permute-start.58 = (bf16[128,3072]{1,0:T(8,128)(2,1)S(1)}, bf16[128,3072]{1,0:T(8,128)(2,1)S(1)}, u32[]{:S(2)}, u32[]{:S(2)}) collective-permute-start(bf16[128,3072]{1,0:T(8,128)(2,1)S(1)} %bitcast.503), channel_id=1, source_target_pairs={{0,4},{4,0},{8,12},{12,8},{16,20},{20,16},{24,28},{28,24},{1,5},{5... | collective-permute-start | bytes 2359304 | tf_op jit(solution)/shard_map/ppermute | solution.py:24
  (102 other events, 1142.6 us)

commit v2 on v1

--- a/solution.py
+++ b/solution.py
@@ -56,15 +56,19 @@
 def scatter_product(rows, cols):
     tokens, width = rows.shape
     count = lax.axis_size("fsdp")
-    bits = bits_of("fsdp")
     own = width // count
     mine = own_bit("fsdp", 1)
     split = rows.reshape(tokens, count // 2, 2, own)
     sent = half(split, 2, 1 - mine).reshape(tokens, width // 2)
     kept = half(split, 2, mine).reshape(tokens, width // 2)
     arrived = flip(mm(sent, cols, 0, 0).astype(BF), "fsdp", 1)
-    part = (mm(kept, cols, 0, 0) + arrived.astype(F32)).astype(BF)
-    for bit in bits[1:]:
+    return (mm(kept, cols, 0, 0) + arrived.astype(F32)).astype(BF)
+
+
+def scatter_rest(part):
+    count = lax.axis_size("fsdp")
+    own = part.shape[0] * 2 // count
+    for bit in bits_of("fsdp")[1:]:
         mine = own_bit("fsdp", bit)
         remaining = part.shape[0] // own
         view = part.reshape(remaining // 2, 2, own, -1)
@@ -423,6 +427,8 @@
     inner = inner_f.astype(BF)
     grad_out = cotangent[0]
     down_part = scatter_product(inner, grad_out)
+    grad_out, down_part = lax.optimization_barrier((grad_out, down_part))
+    down_part = scatter_rest(down_part)
     final = (hidden + mm(inner, wdown)).astype(BF)
     inner_grad = mm(grad_out, wdown, 1, 1)
     gate_back, upper_back = pull_gate(inner_grad)
@@ -430,12 +436,18 @@
     upper_back = upper_back.astype(BF)
     gate_part = scatter_product(act2, gate_back)
     upper_part = scatter_product(act2, upper_back)
+    gate_back, upper_back, gate_part, upper_part = lax.optimization_barrier(
+        (gate_back, upper_back, gate_part, upper_part)
+    )
+    gate_part, upper_part = scatter_rest(gate_part), scatter_rest(upper_part)
     act2_grad = mm(gate_back, wgate, 1, 1) + mm(upper_back, wupper, 1, 1)
     hidden_norm_grad, mlp_gain_part = pull_mlp(act2_grad)
     hidden_grad = grad_out.astype(F32) + hidden_norm_grad
     branch_grad = hidden_grad.astype(BF)
     out_part = scatter_product(mixed, branch_grad)
     mixed_grad = mm(branch_grad, wout, 1, 1).astype(BF)
+    mixed_grad, out_part, down_part = lax.optimization_barrier((mixed_grad, out_part, down_part))
+    out_part = scatter_rest(out_part)
     groups = 2 if kvh % 2 == 0 else 1
     count = kvh // groups
     gw = query.shape[1] // kvh
@@ -448,6 +460,8 @@
             query, key_tail, key, value_tail, value, mixed_grad, query_raw, qgain,
             cosine, sine, segq, segk, hd, rows, n * count, count,
         )
+        if n == 0:
+            mixed_grad, gate_part, dkt = lax.optimization_barrier((mixed_grad, gate_part, dkt))
         own = slice(n * count * hd, (n + 1) * count * hd)
         key_own = dk + passed_along(dkt, "fsdp", -1).astype(F32)
         value_back = (dv + passed_along(dvt, "fsdp", -1).astype(F32)).astype(BF)
@@ -455,7 +469,7 @@
         query_gain_part = query_gain_part + qpart
         key_gain_part = key_gain_part + kpart
         together = jnp.concatenate([query_back, key_back, value_back], axis=1)
-        qkv_parts.append(scatter_product(act, together))
+        qkv_parts.append(scatter_rest(scatter_product(act, together)))
         wide = slice(n * count * gw, (n + 1) * count * gw)
         term = (
             mm(query_back, wquery[:, wide], 1, 1)

time: 835 us -> 826 us (0.989)
  waiting for transfers between devices: 402 us -> 381 us
    ppermute x69, waiting for transfers between devices: 402 us -> 381 us  [flip(): return lax.ppermute(value, axis, [(i, i ^ bit) for i in range(count)])]
    ppermute x69, starting transfers between devices: 75.1 us -> 87.4 us  [flip(): return lax.ppermute(value, axis, [(i, i ^ bit) for i in range(count)])]
    unnamed x186 -> x154, local copies, waits for them, and re-layouts: 55.4 us -> 45.1 us
  transfers between devices with their start and end apart: 75 -> 75, of which waited for: 36 -> 39; matrix products, arithmetic and copies ran while one was open for 21% -> 27% of each run, Pallas kernels for 7% -> 8%
where the time goes in v2:
time: 826 us; the launch traced here: 816 us
  waiting for transfers between devices  381 us (46%)
  local copies, waits for them, and re-layouts  105 us (13%)
  matrix products  98.4 us (12%)
  starting transfers between devices  95.2 us (12%)
  other arithmetic  71.9 us (9%)
  Pallas kernels  61.9 us (7%)
    ppermute x69, waiting for transfers between devices, flip(): return lax.ppermute(value, axis, [(i, i ^ bit) for i in range(count)])  381 us
    dot_general x29, matrix products, mm(): lax.dot_general(a, b, (((ca,), (cb,)), ((), ())), preferred_element_type=...  98.4 us
    ppermute x69, starting transfers between devices, flip(): return lax.ppermute(value, axis, [(i, i ^ bit) for i in range(count)])  87.4 us
    unnamed x154, local copies, waits for them, and re-layouts  45.1 us
    another operation x66, other arithmetic, pair(): return jnp.stack([low, high], axis=axis)  38.8 us
    pallas_call x2, Pallas kernels, attend_back_call(): pl.pallas_call(functools.partial(attend_back_kernel, rows), grid=(count,)...  35.3 us
    dynamic_slice x4, local copies, waits for them, and re-layouts, half(): return lax.dynamic_index_in_dim(blocks, which, axis, keepdims=False)  24.4 us
  transfers between devices with their start and end apart: 75, of which 39 were waited for; matrix products, arithmetic and copies ran while one was open for 27% of the time, Pallas kernels for 8%

profile of v2, /device:TPU:0, one launch (start us, length us, event | category | flops | bytes accessed | tf_op | source)
XLA Modules:
  0.0 815.8 jit_solution(2923936434013530988)
XLA Ops:
  11.4 16.6 %collective-permute-done = bf16[1,576]{1,0:T(2,128)(2,1)S(1)} collective-permute-done((bf16[1,576]{1,0:T(2,128)(2,1)S(1)}, bf16[1,576]{1,0:T(2,128)(2,1)S(1)}, u32[]{:S(2)}, u32[]{:S(2)}) %collective-permute-start) | collective-permute-done | bytes 1184 | tf_op jit(solution)/shard_map/ppermute | solution.py:24
  31.6 7.7 collective-permute-done.7
  41.4 9.2 %collective-permute-done.4 = bf16[256,1024]{1,0:T(8,128)(2,1)} collective-permute-done((bf16[256,1024]{1,0:T(8,128)(2,1)}, bf16[256,1024]{1,0:T(8,128)(2,1)}, u32[]{:S(2)}, u32[]{:S(2)}) %collective-permute-start.4) | collective-permute-done | bytes 524320 | tf_op jit(solution)/shard_map/ppermute | solution.py:24
  55.5 17.4 %collective-permute-done.10 = bf16[512,1024]{1,0:T(8,128)(2,1)S(1)} collective-permute-done((bf16[512,1024]{1,0:T(8,128)(2,1)}, bf16[512,1024]{1,0:T(8,128)(2,1)S(1)}, u32[]{:S(2)}, u32[]{:S(2)}) %collective-permute-start.10) | collective-permute-done | bytes 1048608 | tf_op jit(solution)/shard_map/ppermute | solution.py:24
  84.5 22.2 %collective-permute-done.14 = bf16[256,3072]{1,0:T(8,128)(2,1)} collective-permute-done((bf16[256,3072]{1,0:T(8,128)(2,1)}, bf16[256,3072]{1,0:T(8,128)(2,1)}, u32[]{:S(2)}, u32[]{:S(2)}) %collective-permute-start.14) | collective-permute-done | bytes 1572896 | tf_op jit(solution)/shard_map/ppermute | solution.py:24
  108.1 32.2 %collective-permute-done.12 = bf16[256,3072]{1,0:T(8,128)(2,1)S(1)} collective-permute-done((bf16[256,3072]{1,0:T(8,128)(2,1)}, bf16[256,3072]{1,0:T(8,128)(2,1)S(1)}, u32[]{:S(2)}, u32[]{:S(2)}) %collective-permute-start.12) | collective-permute-done | bytes 1572896 | tf_op jit(solution)/shard_map/ppermute | solution.py:24
  146.4 27.3 %collective-permute-done.16 = bf16[768,1024]{1,0:T(8,128)(2,1)S(1)} collective-permute-done((bf16[768,1024]{1,0:T(8,128)(2,1)}, bf16[768,1024]{1,0:T(8,128)(2,1)S(1)}, u32[]{:S(2)}, u32[]{:S(2)}) %collective-permute-start.16) | collective-permute-done | bytes 1572896 | tf_op jit(solution)/shard_map/ppermute | solution.py:24
  188.8 4.8 shard_map.237.q
  193.8 15.7 %shard_map.239 = bf16[512,2048]{1,0:T(8,128)(2,1)S(1)} custom-call(bf16[512,2048]{1,0:T(8,128)(2,1)S(1)} %shard_map.237.q, bf16[512,1024]{1,0:T(8,128)(2,1)S(1)} %collective-permute-done.6.kt, bf16[512,1024]{1,0:T(8,128)(2,1)S(1)} %shard_map.238.k, bf16[512,1024]{1,0:T(8,128)(2,1)S(1)} %collective-permute-done.9.vt, ...), custom_call_target="tpu_custom_call" | custom-call | flops 12884901888 | bytes 8388608 | tf_op jit(solution)/shard_map/pallas_call | solution.py:254
  219.7 4.4 select_bitcast_fusion.5
  227.4 5.5 fusion.91
  232.9 6.1 multiply_convert_fusion.1
  239.1 8.6 %reshape.497 = bf16[512,2,2,768]{3,2,1,0:T(2,128)(2,1)} reshape(bf16[512,3072]{1,0:T(8,128)(2,1)} %get-tuple-element.171) | data formatting | bytes 6291456 | tf_op jit(solution)/shard_map/reshape | solution.py:61
  247.7 11.9 %constant_dynamic-slice_fusion.7 = (bf16[512,2,1,768]{3,2,1,0:T(2,128)(2,1)}, bf16[512,2,1,768]{3,2,1,0:T(2,128)(2,1)}) fusion(bf16[512,2,2,768]{3,2,1,0:T(2,128)(2,1)} %reshape.497, s32[]{:T(128)S(6)} %select_n.740, s32[]{:T(128)S(6)} %select_n.741), kind=kLoop, calls=%fused_computation.260 | loop fusion | bytes 6291464 | tf_op jit(solution)/shard_map/jit(dynamic_index_in_dim)/dynamic_slice | solution.py:53
  259.6 8.2 %copy.66 = bf16[512,2,1,768]{0,3,1,2:T(8,128)(2,1)} copy(bf16[512,2,1,768]{3,2,1,0:T(2,128)(2,1)} %get-tuple-element.86) | data formatting | bytes 3145728
  267.8 5.2 convolution_convert_fusion.2
  276.8 5.1 constant_dynamic-slice_fusion.4
  284.2 8.2 %copy.65 = bf16[512,2,1,768]{0,3,1,2:T(8,128)(2,1)} copy(bf16[512,2,1,768]{3,2,1,0:T(2,128)(2,1)} %get-tuple-element.85) | data formatting | bytes 3145728
  297.7 6.2 add_convert_fusion.2
  303.9 9.5 %multiply_convert_fusion = (bf16[512,3072]{1,0:T(8,128)(2,1)}, bf16[512,3072]{1,0:T(8,128)(2,1)S(1)}) fusion(f32[512,3072]{1,0:T(8,128)} %copy-done.68, f32[512,3072]{1,0:T(8,128)} %get-tuple-element.172, bf16[512,1024]{1,0:T(8,128)(2,1)S(1)} %bitcast.538, bf16[3072,1024]{1,0:T(8,128)(2,1)S(1)} %bitcast.473), kind=kOutput, calls=%fused_computation.9 | convolution fusion | flops 3243245568 | bytes 26214400 | tf_op jit(solution)/shard_map/dot_general | solution.py:19
  313.4 3.5 convolution_convert_fusion.1
  317.0 4.1 reshape.549
  321.1 4.1 copy.63
  325.2 5.6 convolution_convert_fusion
  338.8 3.3 reshape.503
  344.4 6.3 constant_dynamic-slice_fusion.3
  350.7 6.0 copy.70
  356.7 4.6 copy.69
  361.3 8.8 %fusion.28 = bf16[1,512,1024]{2,1,0:T(8,128)(2,1)} fusion(f32[512,1024]{1,0:T(8,128)} %copy-done.25, bf16[512,3072]{1,0:T(8,128)(2,1)} %get-tuple-element.171, bf16[3072,1024]{1,0:T(8,128)(2,1)} %bitcast.474), kind=kOutput, calls=%fused_computation.111 | convolution fusion | flops 3222274048 | bytes 12582912 | tf_op jit(solution)/shard_map/dot_general | solution.py:19
  374.0 5.6 add_convert_fusion.1
  379.6 4.0 add_convert_fusion
  383.7 4.8 fusion.92
  388.5 5.6 multiply_reduce_fusion
  402.8 28.8 %collective-permute-done.62 = bf16[1,256,3072]{2,1,0:T(8,128)(2,1)S(1)} collective-permute-done((bf16[1,256,3072]{2,1,0:T(8,128)(2,1)S(1)}, bf16[1,256,3072]{2,1,0:T(8,128)(2,1)S(1)}, u32[]{:S(2)}, u32[]{:S(2)}) %collective-permute-start.62) | collective-permute-done | bytes 1572896 | tf_op jit(solution)/shard_map/ppermute | solution.py:24
  434.7 28.7 %collective-permute-done.23 = bf16[1,256,3072]{2,1,0:T(8,128)(2,1)S(1)} collective-permute-done((bf16[1,256,3072]{2,1,0:T(8,128)(2,1)S(1)}, bf16[1,256,3072]{2,1,0:T(8,128)(2,1)S(1)}, u32[]{:S(2)}, u32[]{:S(2)}) %collective-permute-start.23) | collective-permute-done | bytes 1572896 | tf_op jit(solution)/shard_map/ppermute | solution.py:24
  468.2 17.5 %shard_map.240 = (bf16[512,1024]{1,0:T(8,128)(2,1)S(1)}, f32[1,128]{1,0:T(1,128)S(1)}, bf16[512,512]{1,0:T(8,128)(2,1)S(1)}, f32[512,512]{1,0:T(8,128)S(1)}, bf1...) custom-call(bf16[512,2048]{1,0:T(8,128)(2,1)S(1)} %copy-done.4, bf16[512,1024]{1,0:T(8,128)(2,1)S(1)} %copy-done.11, ...), custom_call_target="tpu_custom_call" | custom-call | flops 10737418240 | bytes 10485760 | tf_op jit(solution)/shard_map/pallas_call | solution.py:328
  485.7 17.7 %shard_map.242 = (bf16[512,1024]{1,0:T(8,128)(2,1)S(1)}, f32[1,128]{1,0:T(1,128)S(1)}, bf16[512,512]{1,0:T(8,128)(2,1)S(1)}, f32[512,512]{1,0:T(8,128)S(1)}, bf1...) custom-call(bf16[512,2048]{1,0:T(8,128)(2,1)S(1)} %copy-done.4, bf16[512,1024]{1,0:T(8,128)(2,1)S(1)} %copy-done.11, ...), custom_call_target="tpu_custom_call" | custom-call | flops 10737418240 | bytes 10485760 | tf_op jit(solution)/shard_map/pallas_call | solution.py:328
  519.1 4.6 collective-permute-start.49
  538.6 4.7 collective-permute-start.28
  545.1 8.5 %collective-permute-done.29 = f32[2304]{0:T(1024)S(1)} collective-permute-done((f32[2304]{0:T(1024)S(1)}, f32[2304]{0:T(1024)S(1)}, u32[]{:S(2)}, u32[]{:S(2)}) %collective-permute-start.29) | collective-permute-done | bytes 9248 | tf_op jit(solution)/shard_map/ppermute | solution.py:24
  556.9 6.0 collective-permute-done.30
  577.1 8.0 collective-permute-done.65
  585.8 3.4 collective-permute-start.66
  589.6 8.9 %collective-permute-done.66 = bf16[32,3072]{1,0:T(8,128)(2,1)S(1)} collective-permute-done((bf16[32,3072]{1,0:T(8,128)(2,1)S(1)}, bf16[32,3072]{1,0:T(8,128)(2,1)S(1)}, u32[]{:S(2)}, u32[]{:S(2)}) %collective-permute-start.66) | collective-permute-done | bytes 196640 | tf_op jit(solution)/shard_map/ppermute | solution.py:24
  598.5 4.1 collective-permute-start.70
  606.2 6.4 collective-permute-done.70
  614.1 9.2 %collective-permute-done.58 = bf16[32,3072]{1,0:T(8,128)(2,1)S(1)} collective-permute-done((bf16[32,3072]{1,0:T(8,128)(2,1)S(1)}, bf16[32,3072]{1,0:T(8,128)(2,1)S(1)}, u32[]{:S(2)}, u32[]{:S(2)}) %collective-permute-start.58) | collective-permute-done | bytes 196640 | tf_op jit(solution)/shard_map/ppermute | solution.py:24
  623.3 3.5 collective-permute-start.71
  626.8 7.5 collective-permute-done.71
  637.6 11.0 %collective-permute-done.59 = bf16[32,3072]{1,0:T(8,128)(2,1)S(1)} collective-permute-done((bf16[32,3072]{1,0:T(8,128)(2,1)S(1)}, bf16[32,3072]{1,0:T(8,128)(2,1)S(1)}, u32[]{:S(2)}, u32[]{:S(2)}) %collective-permute-start.59) | collective-permute-done | bytes 196640 | tf_op jit(solution)/shard_map/ppermute | solution.py:24
  652.8 13.9 %collective-permute-done.51 = bf16[128,1024]{1,0:T(8,128)(2,1)S(1)} collective-permute-done((bf16[128,1024]{1,0:T(8,128)(2,1)S(1)}, bf16[128,1024]{1,0:T(8,128)(2,1)S(1)}, u32[]{:S(2)}, u32[]{:S(2)}) %collective-permute-start.51) | collective-permute-done | bytes 262176 | tf_op jit(solution)/shard_map/ppermute | solution.py:24
  670.3 9.2 %collective-permute-done.73 = bf16[192,1024]{1,0:T(8,128)(2,1)S(1)} collective-permute-done((bf16[192,1024]{1,0:T(8,128)(2,1)S(1)}, bf16[192,1024]{1,0:T(8,128)(2,1)S(1)}, u32[]{:S(2)}, u32[]{:S(2)}) %collective-permute-start.73) | collective-permute-done | bytes 393248 | tf_op jit(solution)/shard_map/ppermute | solution.py:24
  682.6 6.9 collective-permute-done.53
  693.1 5.1 collective-permute-done.54
  706.7 10.7 %collective-permute-done.74 = bf16[384,1024]{1,0:T(8,128)(2,1)S(1)} collective-permute-done((bf16[384,1024]{1,0:T(8,128)(2,1)S(1)}, bf16[384,1024]{1,0:T(8,128)(2,1)S(1)}, u32[]{:S(2)}, u32[]{:S(2)}) %collective-permute-start.74) | collective-permute-done | bytes 786464 | tf_op jit(solution)/shard_map/ppermute | solution.py:24
  719.9 7.1 collective-permute-done.55
  731.1 14.8 %collective-permute-done.34 = bf16[1,256,2048]{2,1,0:T(8,128)(2,1)S(1)} collective-permute-done((bf16[1,256,2048]{2,1,0:T(8,128)(2,1)S(1)}, bf16[1,256,2048]{2,1,0:T(8,128)(2,1)S(1)}, u32[]{:S(2)}, u32[]{:S(2)}) %collective-permute-start.34) | collective-permute-done | bytes 1048608 | tf_op jit(solution)/shard_map/ppermute | solution.py:24
  749.0 8.5 %collective-permute-done.35 = bf16[128,2048]{1,0:T(8,128)(2,1)S(1)} collective-permute-done((bf16[128,2048]{1,0:T(8,128)(2,1)S(1)}, bf16[128,2048]{1,0:T(8,128)(2,1)S(1)}, u32[]{:S(2)}, u32[]{:S(2)}) %collective-permute-start.35) | collective-permute-done | bytes 524320 | tf_op jit(solution)/shard_map/ppermute | solution.py:24
  760.1 5.2 collective-permute-done.36
  770.1 6.9 collective-permute-done.37
  780.0 4.0 collective-permute-done.38
  784.1 5.5 collective-permute-done.47
  794.8 9.9 %collective-permute-done.48 = bf16[128,2048]{1,0:T(8,128)(2,1)S(1)} collective-permute-done((bf16[128,2048]{1,0:T(8,128)(2,1)S(1)}, bf16[128,2048]{1,0:T(8,128)(2,1)S(1)}, u32[]{:S(2)}, u32[]{:S(2)}) %collective-permute-start.48) | collective-permute-done | bytes 524320 | tf_op jit(solution)/shard_map/ppermute | solution.py:24
  806.5 3.8 collective-permute-done.40
  (458 shorter events, 224.4 us)
Async XLA Ops:
  0.7 53.7 %collective-permute-start.2 = (bf16[256,2048]{1,0:T(8,128)(2,1)}, bf16[256,2048]{1,0:T(8,128)(2,1)S(1)}, u32[]{:S(2)}, u32[]{:S(2)}) collective-permute-start(bf16[256,2048]{1,0:T(8,128)(2,1)} %param.18), channel_id=1, source_target_pairs={{0,2},{1,3},{2,0},{3,1},{4,6},{5,7},{6,4},{7,5},{8,10},{9,11},{10,... | collective-permute-start | bytes 3145736 | tf_op jit(solution)/shard_map/ppermute | solution.py:24
  4.5 23.5 %collective-permute-start = (bf16[1,576]{1,0:T(2,128)(2,1)S(1)}, bf16[1,576]{1,0:T(2,128)(2,1)S(1)}, u32[]{:S(2)}, u32[]{:S(2)}) collective-permute-start(bf16[1,576]{1,0:T(2,128)(2,1)S(1)} %broadcast_in_dim.14), channel_id=1, source_target_pairs={{0,2},{1,3},{2,0},{3,1},{4,6},{5,7},{6,4},{7,5},{8,10},{9,11},{10,... | collective-permute-start | bytes 3464 | tf_op jit(solution)/shard_map/ppermute | solution.py:24
  4.5 34.8 %collective-permute-start.7 = (bf16[256,1024]{1,0:T(8,128)(2,1)}, bf16[256,1024]{1,0:T(8,128)(2,1)}, u32[]{:S(2)}, u32[]{:S(2)}) collective-permute-start(bf16[256,1024]{1,0:T(8,128)(2,1)} %param.20), channel_id=1, source_target_pairs={{0,2},{1,3},{2,0},{3,1},{4,6},{5,7},{6,4},{7,5},{8,10},{9,11},{10,... | collective-permute-start | bytes 1572872 | tf_op jit(solution)/shard_map/ppermute | solution.py:24
  6.5 44.0 %collective-permute-start.4 = (bf16[256,1024]{1,0:T(8,128)(2,1)}, bf16[256,1024]{1,0:T(8,128)(2,1)}, u32[]{:S(2)}, u32[]{:S(2)}) collective-permute-start(bf16[256,1024]{1,0:T(8,128)(2,1)} %param.19), channel_id=1, source_target_pairs={{0,2},{1,3},{2,0},{3,1},{4,6},{5,7},{6,4},{7,5},{8,10},{9,11},{10,... | collective-permute-start | bytes 1572872 | tf_op jit(solution)/shard_map/ppermute | solution.py:24
  6.6 66.3 %collective-permute-start.10 = (bf16[512,1024]{1,0:T(8,128)(2,1)}, bf16[512,1024]{1,0:T(8,128)(2,1)S(1)}, u32[]{:S(2)}, u32[]{:S(2)}) collective-permute-start(bf16[512,1024]{1,0:T(8,128)(2,1)} %param.23), channel_id=1, source_target_pairs={{0,2},{1,3},{2,0},{3,1},{4,6},{5,7},{6,4},{7,5},{8,10},{9,11},{10,... | collective-permute-start | bytes 3145736 | tf_op jit(solution)/shard_map/ppermute | solution.py:24
  29.2 77.5 %collective-permute-start.14 = (bf16[256,3072]{1,0:T(8,128)(2,1)}, bf16[256,3072]{1,0:T(8,128)(2,1)}, u32[]{:S(2)}, u32[]{:S(2)}) collective-permute-start(bf16[256,3072]{1,0:T(8,128)(2,1)} %param.26), channel_id=1, source_target_pairs={{0,2},{1,3},{2,0},{3,1},{4,6},{5,7},{6,4},{7,5},{8,10},{9,11},{10,... | collective-permute-start | bytes 4718600 | tf_op jit(solution)/shard_map/ppermute | solution.py:24
  39.3 101.0 %collective-permute-start.12 = (bf16[256,3072]{1,0:T(8,128)(2,1)}, bf16[256,3072]{1,0:T(8,128)(2,1)S(1)}, u32[]{:S(2)}, u32[]{:S(2)}) collective-permute-start(bf16[256,3072]{1,0:T(8,128)(2,1)} %param.25), channel_id=1, source_target_pairs={{0,2},{1,3},{2,0},{3,1},{4,6},{5,7},{6,4},{7,5},{8,10},{9,11},{10,... | collective-permute-start | bytes 4718600 | tf_op jit(solution)/shard_map/ppermute | solution.py:24
  50.5 123.2 %collective-permute-start.16 = (bf16[768,1024]{1,0:T(8,128)(2,1)}, bf16[768,1024]{1,0:T(8,128)(2,1)S(1)}, u32[]{:S(2)}, u32[]{:S(2)}) collective-permute-start(bf16[768,1024]{1,0:T(8,128)(2,1)} %param.27), channel_id=1, source_target_pairs={{0,2},{1,3},{2,0},{3,1},{4,6},{5,7},{6,4},{7,5},{8,10},{9,11},{10,... | collective-permute-start | bytes 4718600 | tf_op jit(solution)/shard_map/ppermute | solution.py:24
  54.4 21.9 %collective-permute-start.8 = (bf16[2,256,1024]{2,1,0:T(8,128)(2,1)S(1)}, bf16[2,256,1024]{2,1,0:T(8,128)(2,1)S(1)}, u32[]{:S(2)}, u32[]{:S(2)}) collective-permute-start(bf16[2,256,1024]{2,1,0:T(8,128)(2,1)S(1)} %pad_maximum_fusion.19), channel_id=1, source_target_pairs={{0,1},{1,0},{2,3},{3,2},{4,5},{5,4},{6,7},{7,6},{8,9},{9,8},{10,11... | collective-permute-start | bytes 3145736 | tf_op jit(solution)/shard_map/ppermute | solution.py:24
  76.2 105.3 %collective-permute-start.3 = (bf16[2,256,2048]{2,1,0:T(8,128)(2,1)}, bf16[2,256,2048]{2,1,0:T(8,128)(2,1)}, u32[]{:S(2)}, u32[]{:S(2)}) collective-permute-start(bf16[2,256,2048]{2,1,0:T(8,128)(2,1)} %pad_maximum_fusion.8), channel_id=1, source_target_pairs={{0,1},{1,0},{2,3},{3,2},{4,5},{5,4},{6,7},{7,6},{8,9},{9,8},{10,11... | collective-permute-start | bytes 6291464 | tf_op jit(solution)/shard_map/ppermute | solution.py:24
  77.3 132.3 %collective-permute-start.11 = (bf16[2,512,1024]{2,1,0:T(8,128)(2,1)}, bf16[2,512,1024]{2,1,0:T(8,128)(2,1)}, u32[]{:S(2)}, u32[]{:S(2)}) collective-permute-start(bf16[2,512,1024]{2,1,0:T(8,128)(2,1)} %pad_maximum_fusion.11), channel_id=1, source_target_pairs={{0,1},{1,0},{2,3},{3,2},{4,5},{5,4},{6,7},{7,6},{8,9},{9,8},{10,11... | collective-permute-start | bytes 6291464 | tf_op jit(solution)/shard_map/ppermute | solution.py:24
  106.7 87.0 %collective-permute-start.6 = (bf16[512,1024]{1,0:T(8,128)(2,1)S(1)}, bf16[512,1024]{1,0:T(8,128)(2,1)S(1)}, u32[]{:S(2)}, u32[]{:S(2)}) collective-permute-start(bf16[512,1024]{1,0:T(8,128)(2,1)S(1)} %shard_map.238.k), channel_id=1, source_target_pairs={{0,1},{1,2},{2,3},{4,5},{5,6},{6,7},{8,9},{9,10},{10,11},{12,13},{... | collective-permute-start | bytes 3145736 | tf_op jit(solution)/shard_map/ppermute | solution.py:106
  140.3 53.5 %collective-permute-start.9 = (bf16[512,1024]{1,0:T(8,128)(2,1)S(1)}, bf16[512,1024]{1,0:T(8,128)(2,1)S(1)}, u32[]{:S(2)}, u32[]{:S(2)}) collective-permute-start(bf16[512,1024]{1,0:T(8,128)(2,1)S(1)} %convolution_convert_fusion.7.v), channel_id=1, source_target_pairs={{0,1},{1,2},{2,3},{4,5},{5,6},{6,7},{8,9},{9,10},{10,11},{12,13},{... | collective-permute-start | bytes 3145736 | tf_op jit(solution)/shard_map/ppermute | solution.py:106
  174.8 44.9 %collective-permute-start.13 = (bf16[2,256,3072]{2,1,0:T(8,128)(2,1)}, bf16[2,256,3072]{2,1,0:T(8,128)(2,1)}, u32[]{:S(2)}, u32[]{:S(2)}) collective-permute-start(bf16[2,256,3072]{2,1,0:T(8,128)(2,1)} %pad_maximum_fusion.5), channel_id=1, source_target_pairs={{0,1},{1,0},{2,3},{3,2},{4,5},{5,4},{6,7},{7,6},{8,9},{9,8},{10,11... | collective-permute-start | bytes 9437192 | tf_op jit(solution)/shard_map/ppermute | solution.py:24
  181.5 35.0 %collective-permute-start.15 = (bf16[2,256,3072]{2,1,0:T(8,128)(2,1)}, bf16[2,256,3072]{2,1,0:T(8,128)(2,1)}, u32[]{:S(2)}, u32[]{:S(2)}) collective-permute-start(bf16[2,256,3072]{2,1,0:T(8,128)(2,1)} %pad_maximum_fusion.6), channel_id=1, source_target_pairs={{0,1},{1,0},{2,3},{3,2},{4,5},{5,4},{6,7},{7,6},{8,9},{9,8},{10,11... | collective-permute-start | bytes 9437192 | tf_op jit(solution)/shard_map/ppermute | solution.py:24
  193.7 98.7 %collective-permute-start.17 = (bf16[2,768,1024]{2,1,0:T(8,128)(2,1)}, bf16[2,768,1024]{2,1,0:T(8,128)(2,1)}, u32[]{:S(2)}, u32[]{:S(2)}) collective-permute-start(bf16[2,768,1024]{2,1,0:T(8,128)(2,1)} %pad_maximum_fusion.7), channel_id=1, source_target_pairs={{0,1},{1,0},{2,3},{3,2},{4,5},{5,4},{6,7},{7,6},{8,9},{9,8},{10,11... | collective-permute-start | bytes 9437192 | tf_op jit(solution)/shard_map/ppermute | solution.py:24
  273.0 23.3 %collective-permute-start.18 = (bf16[1536,1024]{1,0:T(8,128)(2,1)}, bf16[1536,1024]{1,0:T(8,128)(2,1)}, u32[]{:S(2)}, u32[]{:S(2)}) collective-permute-start(bf16[1536,1024]{1,0:T(8,128)(2,1)} %convolution_convert_fusion.2), channel_id=1, source_target_pairs={{0,1},{1,0},{2,3},{3,2},{4,5},{5,4},{6,7},{7,6},{8,9},{9,8},{10,11... | collective-permute-start | bytes 9437192 | tf_op jit(solution)/shard_map/ppermute | solution.py:24
  317.0 57.0 %collective-permute-start.19 = (bf16[512,3072]{1,0:T(8,128)(2,1)}, bf16[512,3072]{1,0:T(8,128)(2,1)}, u32[]{:S(2)}, u32[]{:S(2)}) collective-permute-start(bf16[512,3072]{1,0:T(8,128)(2,1)} %convolution_convert_fusion.1), channel_id=1, source_target_pairs={{0,1},{1,0},{2,3},{3,2},{4,5},{5,4},{6,7},{7,6},{8,9},{9,8},{10,11... | collective-permute-start | bytes 9437192 | tf_op jit(solution)/shard_map/ppermute | solution.py:24
  330.8 48.8 %collective-permute-start.20 = (bf16[512,3072]{1,0:T(8,128)(2,1)}, bf16[512,3072]{1,0:T(8,128)(2,1)}, u32[]{:S(2)}, u32[]{:S(2)}) collective-permute-start(bf16[512,3072]{1,0:T(8,128)(2,1)} %convolution_convert_fusion), channel_id=1, source_target_pairs={{0,1},{1,0},{2,3},{3,2},{4,5},{5,4},{6,7},{7,6},{8,9},{9,8},{10,11... | collective-permute-start | bytes 9437192 | tf_op jit(solution)/shard_map/ppermute | solution.py:24
  334.1 37.7 %collective-permute-start.22 = (bf16[1,768,1024]{2,1,0:T(8,128)(2,1)}, bf16[1,768,1024]{2,1,0:T(8,128)(2,1)}, u32[]{:S(2)}, u32[]{:S(2)}) collective-permute-start(bf16[1,768,1024]{2,1,0:T(8,128)(2,1)} %dynamic-slice_bitcast_fusion.2), channel_id=1, source_target_pairs={{0,2},{1,3},{2,0},{3,1},{4,6},{5,7},{6,4},{7,5},{8,10},{9,11},{10,... | collective-permute-start | bytes 4718600 | tf_op jit(solution)/shard_map/ppermute | solution.py:24
  394.2 37.4 %collective-permute-start.62 = (bf16[1,256,3072]{2,1,0:T(8,128)(2,1)S(1)}, bf16[1,256,3072]{2,1,0:T(8,128)(2,1)S(1)}, u32[]{:S(2)}, u32[]{:S(2)}) collective-permute-start(bf16[1,256,3072]{2,1,0:T(8,128)(2,1)S(1)} %dynamic-slice_bitcast_fusion), channel_id=1, source_target_pairs={{0,2},{1,3},{2,0},{3,1},{4,6},{5,7},{6,4},{7,5},{8,10},{9,11},{10,... | collective-permute-start | bytes 4718600 | tf_op jit(solution)/shard_map/ppermute | solution.py:24
  398.5 65.6 %collective-permute-start.21 = (bf16[1024,1024]{1,0:T(8,128)(2,1)S(1)}, bf16[1024,1024]{1,0:T(8,128)(2,1)S(1)}, u32[]{:S(2)}, u32[]{:S(2)}) collective-permute-start(bf16[1024,1024]{1,0:T(8,128)(2,1)S(1)} %convolution_convert_fusion.6), channel_id=1, source_target_pairs={{0,1},{1,0},{2,3},{3,2},{4,5},{5,4},{6,7},{7,6},{8,9},{9,8},{10,11... | collective-permute-start | bytes 6291464 | tf_op jit(solution)/shard_map/ppermute | solution.py:24
  399.2 64.2 %collective-permute-start.23 = (bf16[1,256,3072]{2,1,0:T(8,128)(2,1)S(1)}, bf16[1,256,3072]{2,1,0:T(8,128)(2,1)S(1)}, u32[]{:S(2)}, u32[]{:S(2)}) collective-permute-start(bf16[1,256,3072]{2,1,0:T(8,128)(2,1)S(1)} %dynamic-slice_bitcast_fusion.1), channel_id=1, source_target_pairs={{0,2},{1,3},{2,0},{3,1},{4,6},{5,7},{6,4},{7,5},{8,10},{9,11},{10,... | collective-permute-start | bytes 4718600 | tf_op jit(solution)/shard_map/ppermute | solution.py:24
  433.2 85.0 %collective-permute-start.63 = (bf16[128,3072]{1,0:T(8,128)(2,1)}, bf16[128,3072]{1,0:T(8,128)(2,1)S(1)}, u32[]{:S(2)}, u32[]{:S(2)}) collective-permute-start(bf16[128,3072]{1,0:T(8,128)(2,1)} %dynamic-slice_bitcast_fusion.7), channel_id=1, source_target_pairs={{0,4},{4,0},{8,12},{12,8},{16,20},{20,16},{24,28},{28,24},{1,5},{5... | collective-permute-start | bytes 2359304 | tf_op jit(solution)/shard_map/ppermute | solution.py:24
  503.5 31.7 %collective-permute-start.27 = (bf16[512,512]{1,0:T(8,128)(2,1)S(1)}, bf16[512,512]{1,0:T(8,128)(2,1)}, u32[]{:S(2)}, u32[]{:S(2)}) collective-permute-start(bf16[512,512]{1,0:T(8,128)(2,1)S(1)} %get-tuple-element.60), channel_id=1, source_target_pairs={{1,0},{2,1},{3,2},{5,4},{6,5},{7,6},{9,8},{10,9},{11,10},{13,12},{... | collective-permute-start | bytes 1572872 | tf_op jit(solution)/shard_map/ppermute | solution.py:106
  504.8 20.3 %collective-permute-start.26 = (bf16[512,512]{1,0:T(8,128)(2,1)S(1)}, bf16[512,512]{1,0:T(8,128)(2,1)S(1)}, u32[]{:S(2)}, u32[]{:S(2)}) collective-permute-start(bf16[512,512]{1,0:T(8,128)(2,1)S(1)} %get-tuple-element.57), channel_id=1, source_target_pairs={{1,0},{2,1},{3,2},{5,4},{6,5},{7,6},{9,8},{10,9},{11,10},{13,12},{... | collective-permute-start | bytes 1572872 | tf_op jit(solution)/shard_map/ppermute | solution.py:106
  506.1 23.2 %collective-permute-start.25 = (bf16[512,512]{1,0:T(8,128)(2,1)S(1)}, bf16[512,512]{1,0:T(8,128)(2,1)S(1)}, u32[]{:S(2)}, u32[]{:S(2)}) collective-permute-start(bf16[512,512]{1,0:T(8,128)(2,1)S(1)} %get-tuple-element.53), channel_id=1, source_target_pairs={{1,0},{2,1},{3,2},{5,4},{6,5},{7,6},{9,8},{10,9},{11,10},{13,12},{... | collective-permute-start | bytes 1572872 | tf_op jit(solution)/shard_map/ppermute | solution.py:106
  507.4 23.5 %collective-permute-start.24 = (bf16[512,512]{1,0:T(8,128)(2,1)S(1)}, bf16[512,512]{1,0:T(8,128)(2,1)}, u32[]{:S(2)}, u32[]{:S(2)}) collective-permute-start(bf16[512,512]{1,0:T(8,128)(2,1)S(1)} %get-tuple-element.50), channel_id=1, source_target_pairs={{1,0},{2,1},{3,2},{5,4},{6,5},{7,6},{9,8},{10,9},{11,10},{13,12},{... | collective-permute-start | bytes 1572872 | tf_op jit(solution)/shard_map/ppermute | solution.py:106
  519.1 83.6 %collective-permute-start.49 = (bf16[1,512,1024]{2,1,0:T(8,128)(2,1)}, bf16[1,512,1024]{2,1,0:T(8,128)(2,1)}, u32[]{:S(2)}, u32[]{:S(2)}) collective-permute-start(bf16[1,512,1024]{2,1,0:T(8,128)(2,1)} %dynamic-slice_bitcast_fusion.3), channel_id=1, source_target_pairs={{0,2},{1,3},{2,0},{3,1},{4,6},{5,7},{6,4},{7,5},{8,10},{9,11},{10,... | collective-permute-start | bytes 3145736 | tf_op jit(solution)/shard_map/ppermute | solution.py:24
  525.1 48.0 %collective-permute-start.56 = (bf16[128,3072]{1,0:T(8,128)(2,1)}, bf16[128,3072]{1,0:T(8,128)(2,1)}, u32[]{:S(2)}, u32[]{:S(2)}) collective-permute-start(bf16[128,3072]{1,0:T(8,128)(2,1)} %dynamic-slice_bitcast_fusion.8), channel_id=1, source_target_pairs={{0,4},{4,0},{8,12},{12,8},{16,20},{20,16},{24,28},{28,24},{1,5},{5... | collective-permute-start | bytes 2359304 | tf_op jit(solution)/shard_map/ppermute | solution.py:24
  529.3 56.5 %collective-permute-start.69 = (bf16[384,1024]{1,0:T(8,128)(2,1)}, bf16[384,1024]{1,0:T(8,128)(2,1)S(1)}, u32[]{:S(2)}, u32[]{:S(2)}) collective-permute-start(bf16[384,1024]{1,0:T(8,128)(2,1)} %dynamic-slice_bitcast_fusion.6), channel_id=1, source_target_pairs={{0,4},{4,0},{8,12},{12,8},{16,20},{20,16},{24,28},{28,24},{1,5},{5... | collective-permute-start | bytes 2359304 | tf_op jit(solution)/shard_map/ppermute | solution.py:24
  543.3 29.1 %collective-permute-start.64 = (bf16[64,3072]{1,0:T(8,128)(2,1)S(1)}, bf16[64,3072]{1,0:T(8,128)(2,1)S(1)}, u32[]{:S(2)}, u32[]{:S(2)}) collective-permute-start(bf16[64,3072]{1,0:T(8,128)(2,1)S(1)} %dynamic-slice_bitcast_fusion.13), channel_id=1, source_target_pairs={{0,8},{4,12},{8,0},{12,4},{16,24},{20,28},{24,16},{28,20},{1,9},{5... | collective-permute-start | bytes 1179656 | tf_op jit(solution)/shard_map/ppermute | solution.py:24
  553.6 9.3 %collective-permute-start.30 = (f32[2304]{0:T(1024)S(1)}, f32[2304]{0:T(1024)S(1)}, u32[]{:S(2)}, u32[]{:S(2)}) collective-permute-start(f32[2304]{0:T(1024)S(1)} %add.429), channel_id=1, source_target_pairs={{0,4},{4,0},{8,12},{12,8},{16,20},{20,16},{24,28},{28,24},{1,5},{5... | collective-permute-start | bytes 27656 | tf_op jit(solution)/shard_map/ppermute | solution.py:24
  571.2 127.9 %collective-permute-start.41 = (bf16[512,2048]{1,0:T(8,128)(2,1)S(1)}, bf16[512,2048]{1,0:T(8,128)(2,1)S(1)}, u32[]{:S(2)}, u32[]{:S(2)}) collective-permute-start(bf16[512,2048]{1,0:T(8,128)(2,1)S(1)} %convolution_convert_fusion.4), channel_id=1, source_target_pairs={{0,1},{1,0},{2,3},{3,2},{4,5},{5,4},{6,7},{7,6},{8,9},{9,8},{10,11... | collective-permute-start | bytes 6291464 | tf_op jit(solution)/shard_map/ppermute | solution.py:24
  572.4 128.2 %collective-permute-start.33 = (bf16[512,2048]{1,0:T(8,128)(2,1)S(1)}, bf16[512,2048]{1,0:T(8,128)(2,1)S(1)}, u32[]{:S(2)}, u32[]{:S(2)}) collective-permute-start(bf16[512,2048]{1,0:T(8,128)(2,1)S(1)} %convolution_convert_fusion.5), channel_id=1, source_target_pairs={{0,1},{1,0},{2,3},{3,2},{4,5},{5,4},{6,7},{7,6},{8,9},{9,8},{10,11... | collective-permute-start | bytes 6291464 | tf_op jit(solution)/shard_map/ppermute | solution.py:24
  573.1 12.0 %collective-permute-start.65 = (bf16[32,3072]{1,0:T(8,128)(2,1)S(1)}, bf16[32,3072]{1,0:T(8,128)(2,1)S(1)}, u32[]{:S(2)}, u32[]{:S(2)}) collective-permute-start(bf16[32,3072]{1,0:T(8,128)(2,1)S(1)} %dynamic-slice_bitcast_fusion.19), channel_id=1, source_target_pairs={{0,16},{4,20},{8,24},{12,28},{16,0},{20,4},{24,8},{28,12},{1,17},{... | collective-permute-start | bytes 589832 | tf_op jit(solution)/shard_map/ppermute | solution.py:24
  585.1 19.4 %collective-permute-start.57 = (bf16[64,3072]{1,0:T(8,128)(2,1)S(1)}, bf16[64,3072]{1,0:T(8,128)(2,1)S(1)}, u32[]{:S(2)}, u32[]{:S(2)}) collective-permute-start(bf16[64,3072]{1,0:T(8,128)(2,1)S(1)} %dynamic-slice_bitcast_fusion.14), channel_id=1, source_target_pairs={{0,8},{4,12},{8,0},{12,4},{16,24},{20,28},{24,16},{28,20},{1,9},{5... | collective-permute-start | bytes 1179656 | tf_op jit(solution)/shard_map/ppermute | solution.py:24
  585.8 12.7 %collective-permute-start.66 = (bf16[32,3072]{1,0:T(8,128)(2,1)S(1)}, bf16[32,3072]{1,0:T(8,128)(2,1)S(1)}, u32[]{:S(2)}, u32[]{:S(2)}) collective-permute-start(bf16[32,3072]{1,0:T(8,128)(2,1)S(1)} %fusion.52), channel_id=1, source_target_pairs={{0,16},{4,20},{8,24},{12,28},{16,0},{20,4},{24,8},{28,12},{1,17},{... | collective-permute-start | bytes 589832 | tf_op jit(solution)/shard_map/ppermute | solution.py:24
  598.5 14.1 %collective-permute-start.70 = (bf16[192,1024]{1,0:T(8,128)(2,1)S(1)}, bf16[192,1024]{1,0:T(8,128)(2,1)S(1)}, u32[]{:S(2)}, u32[]{:S(2)}) collective-permute-start(bf16[192,1024]{1,0:T(8,128)(2,1)S(1)} %dynamic-slice_bitcast_fusion.12), channel_id=1, source_target_pairs={{0,8},{4,12},{8,0},{12,4},{16,24},{20,28},{24,16},{28,20},{1,9},{5... | collective-permute-start | bytes 1179656 | tf_op jit(solution)/shard_map/ppermute | solution.py:24
  602.7 31.7 %collective-permute-start.67 = (bf16[64,3072]{1,0:T(8,128)(2,1)S(1)}, bf16[64,3072]{1,0:T(8,128)(2,1)S(1)}, u32[]{:S(2)}, u32[]{:S(2)}) collective-permute-start(bf16[64,3072]{1,0:T(8,128)(2,1)S(1)} %bitcast.516), channel_id=1, source_target_pairs={{0,8},{4,12},{8,0},{12,4},{16,24},{20,28},{24,16},{28,20},{1,9},{5... | collective-permute-start | bytes 1179656 | tf_op jit(solution)/shard_map/ppermute | solution.py:24
  604.5 45.7 %collective-permute-start.50 = (bf16[256,1024]{1,0:T(8,128)(2,1)S(1)}, bf16[256,1024]{1,0:T(8,128)(2,1)S(1)}, u32[]{:S(2)}, u32[]{:S(2)}) collective-permute-start(bf16[256,1024]{1,0:T(8,128)(2,1)S(1)} %dynamic-slice_bitcast_fusion.9), channel_id=1, source_target_pairs={{0,4},{4,0},{8,12},{12,8},{16,20},{20,16},{24,28},{28,24},{1,5},{5... | collective-permute-start | bytes 1572872 | tf_op jit(solution)/shard_map/ppermute | solution.py:24
  612.6 10.7 %collective-permute-start.58 = (bf16[32,3072]{1,0:T(8,128)(2,1)S(1)}, bf16[32,3072]{1,0:T(8,128)(2,1)S(1)}, u32[]{:S(2)}, u32[]{:S(2)}) collective-permute-start(bf16[32,3072]{1,0:T(8,128)(2,1)S(1)} %dynamic-slice_bitcast_fusion.20), channel_id=1, source_target_pairs={{0,16},{4,20},{8,24},{12,28},{16,0},{20,4},{24,8},{28,12},{1,17},{... | collective-permute-start | bytes 589832 | tf_op jit(solution)/shard_map/ppermute | solution.py:24
  623.3 11.0 %collective-permute-start.71 = (bf16[96,1024]{1,0:T(8,128)(2,1)S(1)}, bf16[96,1024]{1,0:T(8,128)(2,1)S(1)}, u32[]{:S(2)}, u32[]{:S(2)}) collective-permute-start(bf16[96,1024]{1,0:T(8,128)(2,1)S(1)} %dynamic-slice_bitcast_fusion.18), channel_id=1, source_target_pairs={{0,16},{4,20},{8,24},{12,28},{16,0},{20,4},{24,8},{28,12},{1,17},{... | collective-permute-start | bytes 589832 | tf_op jit(solution)/shard_map/ppermute | solution.py:24
  634.3 14.2 %collective-permute-start.59 = (bf16[32,3072]{1,0:T(8,128)(2,1)S(1)}, bf16[32,3072]{1,0:T(8,128)(2,1)S(1)}, u32[]{:S(2)}, u32[]{:S(2)}) collective-permute-start(bf16[32,3072]{1,0:T(8,128)(2,1)S(1)} %fusion.53), channel_id=1, source_target_pairs={{0,16},{4,20},{8,24},{12,28},{16,0},{20,4},{24,8},{28,12},{1,17},{... | collective-permute-start | bytes 589832 | tf_op jit(solution)/shard_map/ppermute | solution.py:24
  634.4 18.3 %collective-permute-start.72 = (bf16[96,1024]{1,0:T(8,128)(2,1)S(1)}, bf16[96,1024]{1,0:T(8,128)(2,1)S(1)}, u32[]{:S(2)}, u32[]{:S(2)}) collective-permute-start(bf16[96,1024]{1,0:T(8,128)(2,1)S(1)} %fusion.51), channel_id=1, source_target_pairs={{0,16},{4,20},{8,24},{12,28},{16,0},{20,4},{24,8},{28,12},{1,17},{... | collective-permute-start | bytes 589832 | tf_op jit(solution)/shard_map/ppermute | solution.py:24
  648.6 42.0 %collective-permute-start.68 = (bf16[128,3072]{1,0:T(8,128)(2,1)S(1)}, bf16[128,3072]{1,0:T(8,128)(2,1)S(1)}, u32[]{:S(2)}, u32[]{:S(2)}) collective-permute-start(bf16[128,3072]{1,0:T(8,128)(2,1)S(1)} %bitcast.498), channel_id=1, source_target_pairs={{0,4},{4,0},{8,12},{12,8},{16,20},{20,16},{24,28},{28,24},{1,5},{5... | collective-permute-start | bytes 2359304 | tf_op jit(solution)/shard_map/ppermute | solution.py:24
  650.2 16.7 %collective-permute-start.60 = (bf16[64,3072]{1,0:T(8,128)(2,1)S(1)}, bf16[64,3072]{1,0:T(8,128)(2,1)S(1)}, u32[]{:S(2)}, u32[]{:S(2)}) collective-permute-start(bf16[64,3072]{1,0:T(8,128)(2,1)S(1)} %bitcast.517), channel_id=1, source_target_pairs={{0,8},{4,12},{8,0},{12,4},{16,24},{20,28},{24,16},{28,20},{1,9},{5... | collective-permute-start | bytes 1179656 | tf_op jit(solution)/shard_map/ppermute | solution.py:24
  652.7 14.0 %collective-permute-start.51 = (bf16[128,1024]{1,0:T(8,128)(2,1)S(1)}, bf16[128,1024]{1,0:T(8,128)(2,1)S(1)}, u32[]{:S(2)}, u32[]{:S(2)}) collective-permute-start(bf16[128,1024]{1,0:T(8,128)(2,1)S(1)} %dynamic-slice_bitcast_fusion.15), channel_id=1, source_target_pairs={{0,8},{4,12},{8,0},{12,4},{16,24},{20,28},{24,16},{28,20},{1,9},{5... | collective-permute-start | bytes 786440 | tf_op jit(solution)/shard_map/ppermute | solution.py:24
  666.8 12.8 %collective-permute-start.73 = (bf16[192,1024]{1,0:T(8,128)(2,1)S(1)}, bf16[192,1024]{1,0:T(8,128)(2,1)S(1)}, u32[]{:S(2)}, u32[]{:S(2)}) collective-permute-start(bf16[192,1024]{1,0:T(8,128)(2,1)S(1)} %bitcast.518), channel_id=1, source_target_pairs={{0,8},{4,12},{8,0},{12,4},{16,24},{20,28},{24,16},{28,20},{1,9},{5... | collective-permute-start | bytes 1179656 | tf_op jit(solution)/shard_map/ppermute | solution.py:24
  666.9 15.2 %collective-permute-start.52 = (bf16[64,1024]{1,0:T(8,128)(2,1)S(1)}, bf16[64,1024]{1,0:T(8,128)(2,1)S(1)}, u32[]{:S(2)}, u32[]{:S(2)}) collective-permute-start(bf16[64,1024]{1,0:T(8,128)(2,1)S(1)} %dynamic-slice_bitcast_fusion.21), channel_id=1, source_target_pairs={{0,16},{4,20},{8,24},{12,28},{16,0},{20,4},{24,8},{28,12},{1,17},{... | collective-permute-start | bytes 393224 | tf_op jit(solution)/shard_map/ppermute | solution.py:24
  679.5 24.7 %collective-permute-start.61 = (bf16[128,3072]{1,0:T(8,128)(2,1)S(1)}, bf16[128,3072]{1,0:T(8,128)(2,1)S(1)}, u32[]{:S(2)}, u32[]{:S(2)}) collective-permute-start(bf16[128,3072]{1,0:T(8,128)(2,1)S(1)} %bitcast.499), channel_id=1, source_target_pairs={{0,4},{4,0},{8,12},{12,8},{16,20},{20,16},{24,28},{28,24},{1,5},{5... | collective-permute-start | bytes 2359304 | tf_op jit(solution)/shard_map/ppermute | solution.py:24
  689.5 27.9 %collective-permute-start.74 = (bf16[384,1024]{1,0:T(8,128)(2,1)S(1)}, bf16[384,1024]{1,0:T(8,128)(2,1)S(1)}, u32[]{:S(2)}, u32[]{:S(2)}) collective-permute-start(bf16[384,1024]{1,0:T(8,128)(2,1)S(1)} %bitcast.500), channel_id=1, source_target_pairs={{0,4},{4,0},{8,12},{12,8},{16,20},{20,16},{24,28},{28,24},{1,5},{5... | collective-permute-start | bytes 2359304 | tf_op jit(solution)/shard_map/ppermute | solution.py:24
  698.3 28.7 %collective-permute-start.55 = (bf16[256,1024]{1,0:T(8,128)(2,1)S(1)}, bf16[256,1024]{1,0:T(8,128)(2,1)S(1)}, u32[]{:S(2)}, u32[]{:S(2)}) collective-permute-start(bf16[256,1024]{1,0:T(8,128)(2,1)S(1)} %bitcast.501), channel_id=1, source_target_pairs={{0,4},{4,0},{8,12},{12,8},{16,20},{20,16},{24,28},{28,24},{1,5},{5... | collective-permute-start | bytes 1572872 | tf_op jit(solution)/shard_map/ppermute | solution.py:24
  700.5 28.4 %collective-permute-start.42 = (bf16[1,256,2048]{2,1,0:T(8,128)(2,1)S(1)}, bf16[1,256,2048]{2,1,0:T(8,128)(2,1)S(1)}, u32[]{:S(2)}, u32[]{:S(2)}) collective-permute-start(bf16[1,256,2048]{2,1,0:T(8,128)(2,1)S(1)} %dynamic-slice_bitcast_fusion.4), channel_id=1, source_target_pairs={{0,2},{1,3},{2,0},{3,1},{4,6},{5,7},{6,4},{7,5},{8,10},{9,11},{10,... | collective-permute-start | bytes 3145736 | tf_op jit(solution)/shard_map/ppermute | solution.py:24
  702.2 43.7 %collective-permute-start.34 = (bf16[1,256,2048]{2,1,0:T(8,128)(2,1)S(1)}, bf16[1,256,2048]{2,1,0:T(8,128)(2,1)S(1)}, u32[]{:S(2)}, u32[]{:S(2)}) collective-permute-start(bf16[1,256,2048]{2,1,0:T(8,128)(2,1)S(1)} %dynamic-slice_bitcast_fusion.5), channel_id=1, source_target_pairs={{0,2},{1,3},{2,0},{3,1},{4,6},{5,7},{6,4},{7,5},{8,10},{9,11},{10,... | collective-permute-start | bytes 3145736 | tf_op jit(solution)/shard_map/ppermute | solution.py:24
  729.3 18.8 %collective-permute-start.43 = (bf16[128,2048]{1,0:T(8,128)(2,1)S(1)}, bf16[128,2048]{1,0:T(8,128)(2,1)S(1)}, u32[]{:S(2)}, u32[]{:S(2)}) collective-permute-start(bf16[128,2048]{1,0:T(8,128)(2,1)S(1)} %dynamic-slice_bitcast_fusion.10), channel_id=1, source_target_pairs={{0,4},{4,0},{8,12},{12,8},{16,20},{20,16},{24,28},{28,24},{1,5},{5... | collective-permute-start | bytes 1572872 | tf_op jit(solution)/shard_map/ppermute | solution.py:24
  746.4 11.1 %collective-permute-start.35 = (bf16[128,2048]{1,0:T(8,128)(2,1)S(1)}, bf16[128,2048]{1,0:T(8,128)(2,1)S(1)}, u32[]{:S(2)}, u32[]{:S(2)}) collective-permute-start(bf16[128,2048]{1,0:T(8,128)(2,1)S(1)} %dynamic-slice_bitcast_fusion.11), channel_id=1, source_target_pairs={{0,4},{4,0},{8,12},{12,8},{16,20},{20,16},{24,28},{28,24},{1,5},{5... | collective-permute-start | bytes 1572872 | tf_op jit(solution)/shard_map/ppermute | solution.py:24
  748.3 10.3 %collective-permute-start.44 = (bf16[64,2048]{1,0:T(8,128)(2,1)S(1)}, bf16[64,2048]{1,0:T(8,128)(2,1)S(1)}, u32[]{:S(2)}, u32[]{:S(2)}) collective-permute-start(bf16[64,2048]{1,0:T(8,128)(2,1)S(1)} %dynamic-slice_bitcast_fusion.16), channel_id=1, source_target_pairs={{0,8},{4,12},{8,0},{12,4},{16,24},{20,28},{24,16},{28,20},{1,9},{5... | collective-permute-start | bytes 786440 | tf_op jit(solution)/shard_map/ppermute | solution.py:24
  758.7 10.8 %collective-permute-start.45 = (bf16[32,2048]{1,0:T(8,128)(2,1)S(1)}, bf16[32,2048]{1,0:T(8,128)(2,1)S(1)}, u32[]{:S(2)}, u32[]{:S(2)}) collective-permute-start(bf16[32,2048]{1,0:T(8,128)(2,1)S(1)} %dynamic-slice_bitcast_fusion.22), channel_id=1, source_target_pairs={{0,16},{4,20},{8,24},{12,28},{16,0},{20,4},{24,8},{28,12},{1,17},{... | collective-permute-start | bytes 393224 | tf_op jit(solution)/shard_map/ppermute | solution.py:24
  765.4 11.6 %collective-permute-start.37 = (bf16[32,2048]{1,0:T(8,128)(2,1)S(1)}, bf16[32,2048]{1,0:T(8,128)(2,1)S(1)}, u32[]{:S(2)}, u32[]{:S(2)}) collective-permute-start(bf16[32,2048]{1,0:T(8,128)(2,1)S(1)} %dynamic-slice_bitcast_fusion.23), channel_id=1, source_target_pairs={{0,16},{4,20},{8,24},{12,28},{16,0},{20,4},{24,8},{28,12},{1,17},{... | collective-permute-start | bytes 393224 | tf_op jit(solution)/shard_map/ppermute | solution.py:24
  769.5 10.3 %collective-permute-start.46 = (bf16[32,2048]{1,0:T(8,128)(2,1)S(1)}, bf16[32,2048]{1,0:T(8,128)(2,1)S(1)}, u32[]{:S(2)}, u32[]{:S(2)}) collective-permute-start(bf16[32,2048]{1,0:T(8,128)(2,1)S(1)} %fusion.55), channel_id=1, source_target_pairs={{0,16},{4,20},{8,24},{12,28},{16,0},{20,4},{24,8},{28,12},{1,17},{... | collective-permute-start | bytes 393224 | tf_op jit(solution)/shard_map/ppermute | solution.py:24
  779.9 9.7 %collective-permute-start.47 = (bf16[64,2048]{1,0:T(8,128)(2,1)S(1)}, bf16[64,2048]{1,0:T(8,128)(2,1)S(1)}, u32[]{:S(2)}, u32[]{:S(2)}) collective-permute-start(bf16[64,2048]{1,0:T(8,128)(2,1)S(1)} %bitcast.531), channel_id=1, source_target_pairs={{0,8},{4,12},{8,0},{12,4},{16,24},{20,28},{24,16},{28,20},{1,9},{5... | collective-permute-start | bytes 786440 | tf_op jit(solution)/shard_map/ppermute | solution.py:24
  789.7 14.9 %collective-permute-start.48 = (bf16[128,2048]{1,0:T(8,128)(2,1)S(1)}, bf16[128,2048]{1,0:T(8,128)(2,1)S(1)}, u32[]{:S(2)}, u32[]{:S(2)}) collective-permute-start(bf16[128,2048]{1,0:T(8,128)(2,1)S(1)} %bitcast.503), channel_id=1, source_target_pairs={{0,4},{4,0},{8,12},{12,8},{16,20},{20,16},{24,28},{28,24},{1,5},{5... | collective-permute-start | bytes 1572872 | tf_op jit(solution)/shard_map/ppermute | solution.py:24
  793.0 17.3 %collective-permute-start.40 = (bf16[128,2048]{1,0:T(8,128)(2,1)S(1)}, bf16[128,2048]{1,0:T(8,128)(2,1)S(1)}, u32[]{:S(2)}, u32[]{:S(2)}) collective-permute-start(bf16[128,2048]{1,0:T(8,128)(2,1)S(1)} %bitcast.502), channel_id=1, source_target_pairs={{0,4},{4,0},{8,12},{12,8},{16,20},{20,16},{24,28},{28,24},{1,5},{5... | collective-permute-start | bytes 1572872 | tf_op jit(solution)/shard_map/ppermute | solution.py:24
  (85 other events, 994.1 us)
